TPU v7x, 32 devices: a whole 2x2x4 slice. The times are simulated.
32 devices in a mesh: dp: 16 (over z, x, core), fsdp: 2 (over y).
Axes of the slice: x: 2, y: 2, z: 4, core: 2. Of those that a mesh axis runs over, the one named last changes fastest.
Arguments:
- block_input: float32 [32768, 1024], P(('dp', 'fsdp')), may hold values from -6 to 6
- cotangent: float32 [32768, 1024], P(('dp', 'fsdp')), may hold values from -6 to 6
- scene_lengths: int32 [32, 3], P(('dp', 'fsdp')), may hold values from 1 to 480, 960 in all within a row
- norm_gain: float32 [1024], P(('dp', 'fsdp')), may hold values from 0.5 to 1.5
- in_weight: float32 [1024, 4384], P(('dp', 'fsdp')), may hold values from -0.1875 to 0.1875
- conv_weight: float32 [2304, 4], P(('dp', 'fsdp')), may hold values from -3 to 3
- conv_bias: float32 [2304], P(('dp', 'fsdp')), may hold values from -3 to 3
- dt_bias: float32 [32], replicated, may hold values from -7 to -2.3
- a_log: float32 [32], replicated, may hold values from 0 to 2.77
- skip_gain: float32 [32], replicated, may hold values from 0.5 to 1.5
- gated_gain: float32 [2048], P(('dp', 'fsdp')), may hold values from 0.5 to 1.5
- out_weight: float32 [2048, 1024], P(('dp', 'fsdp')), may hold values from -0.125 to 0.125
Outputs:
- block_output: float32 [32768, 1024], P(('dp', 'fsdp'))
- input_grad: float32 [32768, 1024], P(('dp', 'fsdp'))
- norm_gain_grad: float32 [1024], P(('dp', 'fsdp'))
- in_weight_grad: float32 [1024, 4384], P(('dp', 'fsdp'))
- conv_weight_grad: float32 [2304, 4], P(('dp', 'fsdp'))
- conv_bias_grad: float32 [2304], P(('dp', 'fsdp'))
- dt_bias_grad: float32 [32], replicated
- a_log_grad: float32 [32], replicated
- skip_gain_grad: float32 [32], replicated
- gated_gain_grad: float32 [2048], P(('dp', 'fsdp'))
- out_weight_grad: float32 [2048, 1024], P(('dp', 'fsdp'))
Inputs may be any that keep to these rules, and one draw needn't show every extreme that they name: `scene_lengths`: each group's 3 lengths sum to 960 and the longest is exactly 480; the last 64 tokens of every group are padding.
All inputs are finite; a program needn't handle non-finite values.
Results may differ from a plain program's by a relative error of at most 0.012.
Values may be sent and summed in bfloat16 or wider, within the bound.
No kernel may reach another device: no remote copies, remote signals or barrier semaphores. Data moves between devices by JAX's collectives and lax.ppermute only.
A program may use at most 256 MiB of HBM per device.

v0:
```python
import jax
import jax.numpy as jnp
from jax import lax
from jax.sharding import PartitionSpec as P

SPAN = 256


epsilon = 1e-05
highest = lax.Precision.HIGHEST


def rms_scale(matrix, gain):
    return matrix * lax.rsqrt(jnp.mean(matrix * matrix, axis=-1, keepdims=True) + epsilon) * gain


def scene_ids(lengths_row, token_count):
    bounds = jnp.cumsum(lengths_row)
    places = lax.iota(jnp.int32, token_count)
    scene = jnp.sum((places[:, None] >= bounds[None, :]).astype(jnp.int32), axis=1)
    alive = (places < bounds[-1]).astype(jnp.float32)
    return (scene, alive)


def contract(left, right, left_dim, right_dim):
    return lax.dot_general(
        left, right, (((left_dim,), (right_dim,)), ((), ())), preferred_element_type=jnp.float32
    )


def mixer(projected, conv_weight, conv_bias, dt_bias, a_log, skip_gain, gated_gain, scene, alive):
    token_count = projected.shape[0]
    inner_width = gated_gain.shape[0]
    channels = conv_bias.shape[0]
    head_count = a_log.shape[0]
    state_width = (channels - inner_width) // 2
    head_dim = inner_width // head_count
    kernel = conv_weight.shape[1]
    gate_part = projected[:, :inner_width]
    conv_in = projected[:, inner_width : inner_width + channels]
    step_raw = projected[:, inner_width + channels :]
    conv_sum = conv_bias + conv_in * conv_weight[:, kernel - 1]
    for offset in range(1, kernel):
        shifted = jnp.pad(conv_in, ((offset, 0), (0, 0)))[:token_count]
        shifted_scene = jnp.pad(scene, (offset, 0), constant_values=-1)[:token_count]
        same_scene = (shifted_scene == scene).astype(jnp.float32)
        conv_sum = conv_sum + shifted * same_scene[:, None] * conv_weight[:, kernel - 1 - offset]
    activated = jax.nn.silu(conv_sum)
    values = activated[:, :inner_width].reshape(token_count, head_count, head_dim)
    b_in = activated[:, inner_width : inner_width + state_width]
    c_out = activated[:, inner_width + state_width :]
    dt_step = jax.nn.softplus(step_raw + dt_bias)
    log_decay = -dt_step * jnp.exp(a_log)
    block_count = token_count // SPAN
    block_values = values.reshape(block_count, SPAN, head_count, head_dim)
    block_b = b_in.reshape(block_count, SPAN, state_width)
    block_c = c_out.reshape(block_count, SPAN, state_width)
    block_step = jnp.transpose(dt_step.reshape(block_count, SPAN, head_count), (0, 2, 1))
    cum_decay = jnp.transpose(
        jnp.cumsum(log_decay.reshape(block_count, SPAN, head_count), axis=1), (0, 2, 1)
    )
    block_scene = scene.reshape(block_count, SPAN)
    within = lax.iota(jnp.int32, SPAN)
    causal = (
        (within[None, :, None] >= within[None, None, :])
        & (block_scene[:, :, None] == block_scene[:, None, :])
    ).astype(jnp.float32)
    spread = cum_decay[:, :, :, None] - cum_decay[:, :, None, :]
    weights = jnp.exp(jnp.minimum(spread, 0.0)) * causal[:, None, :, :]
    intersection = jnp.einsum("btn,bsn->bts", block_c, block_b, precision=highest)
    scores = weights * intersection[:, None, :, :] * block_step[:, :, None, :]
    inside = jnp.einsum("bhts,bshp->bthp", scores, block_values, precision=highest)
    final_scene = block_scene[:, SPAN - 1]
    prior_scene = jnp.concatenate([jnp.full((1,), -1, jnp.int32), final_scene[:-1]])
    last_cum = cum_decay[:, :, SPAN - 1]
    end_weight = (
        jnp.exp(last_cum[:, :, None] - cum_decay)
        * (block_scene == final_scene[:, None]).astype(jnp.float32)[:, None, :]
        * block_step
    )
    weighted_values = block_values * jnp.transpose(end_weight, (0, 2, 1))[:, :, :, None]
    fresh_state = jnp.einsum("bshp,bsn->bhpn", weighted_values, block_b, precision=highest)
    through = jnp.exp(last_cum) * (final_scene == prior_scene).astype(jnp.float32)[:, None]
    held_state = jnp.zeros((head_count, head_dim, state_width), jnp.float32)
    starting = []
    for number in range(block_count):
        starting.append(held_state)
        held_state = held_state * through[number][:, None, None] + fresh_state[number]
    start_states = jnp.stack(starting)
    entering = (block_scene == prior_scene[:, None]).astype(jnp.float32)
    carry_scale = jnp.transpose(jnp.exp(cum_decay) * entering[:, None, :], (0, 2, 1))
    carried = (
        jnp.einsum("btn,bhpn->bthp", block_c, start_states, precision=highest)
        * carry_scale[:, :, :, None]
    )
    outputs = (inside + carried).reshape(token_count, head_count, head_dim)
    scan_out = outputs + skip_gain[None, :, None] * values
    gated = scan_out.reshape(token_count, inner_width) * jax.nn.silu(gate_part) * alive[:, None]
    return rms_scale(gated, gated_gain)


def local(
    block_input,
    cotangent,
    scene_lengths,
    norm_gain,
    in_weight,
    conv_weight,
    conv_bias,
    dt_bias,
    a_log,
    skip_gain,
    gated_gain,
    out_weight,
):
    gathered = (
        lax.all_gather(norm_gain.astype(jnp.bfloat16), ("dp", "fsdp"), axis=0, tiled=True),
        lax.all_gather(in_weight.astype(jnp.bfloat16), ("dp", "fsdp"), axis=0, tiled=True),
        lax.all_gather(conv_weight.astype(jnp.bfloat16), ("dp", "fsdp"), axis=0, tiled=True),
        lax.all_gather(conv_bias.astype(jnp.bfloat16), ("dp", "fsdp"), axis=0, tiled=True),
        lax.all_gather(gated_gain.astype(jnp.bfloat16), ("dp", "fsdp"), axis=0, tiled=True),
        lax.all_gather(out_weight.astype(jnp.bfloat16), ("dp", "fsdp"), axis=0, tiled=True),
    )
    norm_full, in_full, conv_full, bias_full, gated_full, out_full = gathered
    token_count = block_input.shape[0]
    scene, alive = scene_ids(scene_lengths[0], token_count)
    normed, norm_pull = jax.vjp(rms_scale, block_input, norm_full.astype(jnp.float32))
    normed_low = normed.astype(jnp.bfloat16)
    projected = jnp.dot(normed_low, in_full, preferred_element_type=jnp.float32)

    def local_mix(proj_in, conv_taps, conv_shift, bias_step, decay_log, skip_in, gain_in):
        return mixer(
            proj_in, conv_taps, conv_shift, bias_step, decay_log, skip_in, gain_in, scene, alive
        )

    mixed, mix_pull = jax.vjp(
        local_mix,
        projected,
        conv_full.astype(jnp.float32),
        bias_full.astype(jnp.float32),
        dt_bias,
        a_log,
        skip_gain,
        gated_full.astype(jnp.float32),
    )
    mixed_low = mixed.astype(jnp.bfloat16)
    block_output = block_input + jnp.dot(mixed_low, out_full, preferred_element_type=jnp.float32)
    in_back, out_back = (
        lax.all_gather(in_weight.astype(jnp.bfloat16), ("dp", "fsdp"), axis=0, tiled=True),
        lax.all_gather(out_weight.astype(jnp.bfloat16), ("dp", "fsdp"), axis=0, tiled=True),
    )
    cot_low = cotangent.astype(jnp.bfloat16)
    out_term = contract(mixed_low, cot_low, 0, 0)
    d_mixed = contract(cot_low, out_back, 1, 1)
    d_proj, d_conv, d_shift, d_bias_step, d_decay_log, d_skip, d_gated = mix_pull(d_mixed)
    d_proj_low = d_proj.astype(jnp.bfloat16)
    in_term = contract(normed_low, d_proj_low, 0, 0)
    d_normed = contract(d_proj_low, in_back, 1, 1)
    d_rows, d_gain = norm_pull(d_normed)
    input_grad = cotangent + d_rows
    terms = (d_gain, in_term, d_conv, d_shift, d_gated, out_term)
    summed = (
        lax.psum_scatter(terms[0], ("dp", "fsdp"), scatter_dimension=0, tiled=True),
        lax.psum_scatter(terms[1], ("dp", "fsdp"), scatter_dimension=0, tiled=True),
        lax.psum_scatter(terms[2], ("dp", "fsdp"), scatter_dimension=0, tiled=True),
        lax.psum_scatter(terms[3], ("dp", "fsdp"), scatter_dimension=0, tiled=True),
        lax.psum_scatter(terms[4], ("dp", "fsdp"), scatter_dimension=0, tiled=True),
        lax.psum_scatter(terms[5], ("dp", "fsdp"), scatter_dimension=0, tiled=True),
    )
    gain_grad, in_grad, conv_grad, shift_grad, gated_grad, out_grad = summed
    bias_grad, decay_grad, skip_grad = lax.psum((d_bias_step, d_decay_log, d_skip), ("dp", "fsdp"))
    return (
        block_output,
        input_grad,
        gain_grad,
        in_grad,
        conv_grad,
        shift_grad,
        bias_grad,
        decay_grad,
        skip_grad,
        gated_grad,
        out_grad,
    )


def solution(mesh):
    return jax.shard_map(
        local,
        mesh=mesh,
        in_specs=(
            P(("dp", "fsdp"), None),
            P(("dp", "fsdp"), None),
            P(("dp", "fsdp"), None),
            P(("dp", "fsdp")),
            P(("dp", "fsdp"), None),
            P(("dp", "fsdp"), None),
            P(("dp", "fsdp")),
            P(),
            P(),
            P(),
            P(("dp", "fsdp")),
            P(("dp", "fsdp"), None),
        ),
        out_specs=(
            P(("dp", "fsdp"), None),
            P(("dp", "fsdp"), None),
            P(("dp", "fsdp")),
            P(("dp", "fsdp"), None),
            P(("dp", "fsdp"), None),
            P(("dp", "fsdp")),
            P(),
            P(),
            P(),
            P(("dp", "fsdp")),
            P(("dp", "fsdp"), None),
        ),
        check_vma=False,
    )
```

profile of v0, /device:TPU:0, one launch (start us, length us, event | category | flops | bytes accessed | tf_op | source)
XLA Modules:
  0.0 1017.2 jit_solution(12058902828727902726)
XLA Ops:
  7.2 1.8 convert_element_type.97
  9.1 1.6 convert_element_type.111
  10.8 0.8 reduce-window.16
  12.8 0.7 convert_element_type.92
  13.5 0.7 convert_element_type.108
  14.1 0.7 convert_element_type.94
  15.4 42.6 %all-reduce.34 = (bf16[1024]{0:T(1024)(128)(2,1)S(1)}, bf16[2304]{0:T(1024)(128)(2,1)S(1)}, bf16[2048]{0:T(1024)(128)(2,1)S(1)}) all-reduce(bf16[1024]{0:T(1024)(128)(2,1)S(1)} %dynamic-update-slice.1, bf16[2304]{0:T(1024)(128)(2,1)S(1)} %dynamic-update-slice, ...), channel_id=1, replica_groups=mesh['dp'=16,'fsdp'=2] {'dp','fsdp'}, use_global_device_ids=true, to_apply=%add.27 | all-reduce | flops 5376 | bytes 21504
  58.0 2.5 multiply_reduce_fusion.12
  60.5 0.7 exp.33
  61.2 0.7 convert_bitcast_fusion
  61.9 66.8 %all-gather = bf16[32,72,4]{1,2,0:T(4,128)(2,1)S(1)} all-gather(bf16[1,72,4]{1,2,0:T(4,128)(2,1)S(1)} %convert_bitcast_fusion), channel_id=1, replica_groups=mesh['dp'=16,'fsdp'=2] {'dp','fsdp'}, dimensions={0}, use_global_device_ids=true | all-gather | bytes 19008 | tf_op jit(solution)/shard_map/all_gather | solution.py:119
  129.0 1.2 and_convert_fusion
  130.2 0.7 mul.606
  131.0 0.7 fusion.111
  132.1 17.9 %fusion.124 = f32[1024,4384]{0,1:T(8,128)} fusion(bf16[1024,4384]{1,0:T(8,128)(2,1)} %all-gather.4.cloned.1.call-done, f32[1024,1024]{1,0:T(8,128)} %param.12, f32[1024]{0:T(1024)S(1)} %convert_element_type.95, f32[1024]{0:T(1024)S(1)} %fusion.115), kind=kOutput, calls=%fused_computation.221 | convolution fusion | flops 9197060096 | bytes 31137792 | tf_op jit(solution)/shard_map/dot_general | solution.py:129
  150.0 4.8 slice.129
  154.8 12.5 %fusion.34 = (f32[1024,2304]{0,1:T(8,128)}, f32[1024,2304]{0,1:T(8,128)}) fusion(f32[2304]{0:T(1024)S(1)} %get-tuple-element.31, f32[1024]{0:T(1024)S(1)} %get-tuple-element.78, f32[1024,2304]{0,1:T(8,128)S(1)} %slice.129, f32[2304]{0:T(1024)S(1)} %get-tuple-element.32, f32[1024]{0:T(1024)S(1)} %get-tuple-element.77, f32[2304]{0:T(1024)S(1)} %get-tuple-element.33, ...), kind=kLoop, calls=%fused_computation.53 | loop fusion | flops 35389440 | bytes 28369920 | tf_op jit(solution)/shard_map/jvp(jit(silu))/mul | solution.py:48
  167.3 1.1 negate_multiply_fusion
  168.4 2.3 reduce-window.19
  171.0 8.4 slice.134
  179.4 10.8 %reshape.306 = f32[4,256,32,64]{1,0,3,2:T(4,128)} reshape(f32[1024,2048]{0,1:T(8,128)} %slice.134) | data formatting | bytes 16777216 | tf_op jit(solution)/shard_map/jvp()/reshape;jvp()/reshape | solution.py:55
  190.1 1.3 fusion.131
  193.5 1.0 fusion.132
  194.5 13.6 %fusion.48 = f32[4,32,64,128]{3,2,1,0:T(8,128)S(1)} fusion(f32[4,256,128,1]{2,1,3,0:T(8,128)S(1)} %copy.237, f32[4,256,32,64]{1,0,3,2:T(4,128)} %reshape.306, f32[4,256,32]{1,2,0:T(8,128)S(1)} %get-tuple-element.71), kind=kOutput, calls=%fused_computation.81 | convolution fusion | flops 3223322624 | bytes 13238272 | tf_op jit(solution)/shard_map/jvp(bshp,bsn->bhpn)/dot_general | solution.py:82
  208.5 1.7 copy-done.8
  210.3 7.1 fusion.75
  217.5 3.3 copy-done.6
  220.8 40.5 %bitcast_add_fusion.1 = f32[4,256,32,64]{1,3,2,0:T(8,128)} fusion(f32[4,256,32,64]{1,3,2,0:T(8,128)S(1)} %fusion.75, f32[4,256,32]{1,2,0:T(8,128)S(1)} %get-tuple-element.70, f32[4,32,256]{2,1,0:T(8,128)S(1)} %bitcast.240, f32[4,256,256]{2,1,0:T(8,128)S(1)} %fusion.132, f32[4,256,256]{2,1,0:T(8,128)S(1)} %copy-done.28, ...), kind=kOutput, calls=%fused_computation.62 | convolution fusion | flops 6488588288 | bytes 27656192 | tf_op jit(solution)/shard_map/jvp(bhts,bshp->bthp)/dot_general | solution.py:72
  261.3 14.1 %copy.214 = f32[4,256,32,64]{1,0,3,2:T(4,128)} copy(f32[4,256,32,64]{1,3,2,0:T(8,128)} %bitcast_add_fusion.1) | data formatting | bytes 16777216 | tf_op jit(solution)/shard_map/jvp()/add | solution.py:96
  275.4 5.6 copy.265
  281.1 11.0 %multiply_reduce_fusion.9 = (f32[1024]{0:T(1024)S(1)}, f32[1024,2048]{0,1:T(8,128)}) fusion(f32[1024]{0:T(1024)S(1)} %fusion.111, f32[1024,4384]{0,1:T(8,128)} %fusion.124, f32[1024,2048]{0,1:T(8,128)S(1)} %bitcast.220, f32[1024,2304]{0,1:T(8,128)S(1)} %bitcast.215, f32[2048]{0:T(1024)S(1)} %mul.607), kind=kLoop, calls=%fused_computation.70 | loop fusion | flops 20970496 | bytes 33570816 | tf_op jit(solution)/shard_map/jvp()/reduce_sum | solution.py:14
  292.2 12.2 %multiply_reduce_fusion.4 = (f32[2048]{0:T(1024)}, f32[1024]{0:T(1024)S(1)}, f32[1024,2048]{0,1:T(8,128)S(1)}) fusion(f32[1024,2048]{0,1:T(8,128)} %get-tuple-element.52, f32[1024]{0:T(1024)S(1)} %fusion.116, f32[2048]{0:T(1024)S(1)} %convert_element_type.109, bf16[2048,1024]{1,0:T(8,128)(2,1)} %all-gather.6.cloned.1.call-done, f32[1024,1024]{1,0:T(8,128)} %param.13), kind=kOutput, calls=%fused_computation.63 | convolution fusion | flops 4308595712 | bytes 25190400 | tf_op jit(solution)/shard_map/dot_general | solution.py:26
  304.4 15.4 %multiply_reduce_fusion.5 = (f32[2048]{0:T(1024)}, f32[1024,2048]{0,1:T(8,128)}, f32[1024,2048]{0,1:T(8,128)}) fusion(f32[1024,2304]{0,1:T(8,128)} %get-tuple-element.58, f32[1024,4384]{0,1:T(8,128)} %fusion.124, f32[1024]{0:T(1024)S(1)} %fusion.111, f32[1024,2048]{0,1:T(8,128)S(1)} %copy-done.5, f32[1024]{0:T(1024)S(1)} %multiply_multiply_fusion.5, ...), kind=kLoop, calls=%fused_computation.64 | loop fusion | flops 46135296 | bytes 58757120 | tf_op jit(solution)/shard_map/transpose(jvp())/reduce_sum | solution.py:97
  319.8 10.7 %reshape.314 = f32[4,256,32,64]{1,0,3,2:T(4,128)} reshape(f32[1024,2048]{0,1:T(8,128)} %get-tuple-element.45) | data formatting | bytes 16777216 | tf_op jit(solution)/shard_map/transpose(jvp())/reshape;transpose(jvp())/reshape | solution.py:96
  330.5 13.4 %fusion.44 = f32[4,32,64,128]{3,2,1,0:T(8,128)} fusion(f32[4,256,128,1]{2,1,3,0:T(8,128)S(1)} %copy-done.12, f32[4,256,32,64]{1,0,3,2:T(4,128)} %reshape.314, f32[4,256,32]{1,2,0:T(8,128)S(1)} %copy-done.35), kind=kOutput, calls=%fused_computation.77 | convolution fusion | flops 3223322624 | bytes 13238272 | tf_op jit(solution)/shard_map/transpose(jvp(btn,bhpn->bthp))/dot_general | solution.py:93
  343.9 58.3 %fusion.59 = (f32[4,32,256]{2,1,0:T(8,128)}, f32[4,32,256]{2,1,0:T(8,128)}, f32[4,32,256]{2,1,0:T(8,128)}, f32[4,256,256]{2,1,0:T(8,128)}) fusion(f32[4,32,256]{2,1,0:T(8,128)S(1)} %copy-done.38, f32[4,256,256]{2,1,0:T(8,128)S(1)} %copy-done.29, f32[4,256,256]{2,1,0:T(8,128)S(1)} %copy-done.31, f32[4,32,256]{2,1,0:T(8,128)S(1)} %bitcast.241, ...), kind=kOutput, calls=%fused_computation.93 | convolution fusion | flops 6601474048 | bytes 20578304 | tf_op jit(solution)/shard_map/transpose(jvp(bhts,bshp->bthp))/dot_general | solution.py:72
  402.2 7.1 fusion.87
  409.3 3.4 multiply_add_fusion.3
  412.9 14.8 %multiply_reduce_fusion.7 = (f32[4,256,32]{1,2,0:T(8,128)S(1)}, f32[4,256,32,64]{1,3,2,0:T(8,128)}) fusion(f32[4,256,32,64]{1,0,3,2:T(4,128)} %reshape.306, f32[4,256,128,1]{2,1,3,0:T(8,128)S(1)} %copy.237, f32[1,32,64,128]{3,2,1,0:T(8,128)S(1)} %get-tuple-element.49, f32[1,32,64,128]{3,2,1,0:T(8,128)} %get-tuple-element.50, ...), kind=kOutput, calls=%fused_computation.67 | convolution fusion | flops 3227484160 | bytes 20578304 | tf_op jit(solution)/shard_map/transpose(jvp(bshp,bsn->bhpn))/dot_general | solution.py:82
  428.0 0.9 fusion.86
  429.2 8.6 multiply_reduce_fusion.6
  438.1 10.0 reduce-window.21
  448.4 17.3 %fusion.81 = f32[4,256,128]{2,1,0:T(8,128)S(1)} fusion(f32[1,32,64,128]{3,2,1,0:T(8,128)S(1)} %copy-done.22, f32[1,32,64,128]{3,2,1,0:T(8,128)} %copy-done.23, f32[1,32,64,128]{3,2,1,0:T(8,128)} %copy-done.24, f32[4]{0:T(128)S(1)} %copy-done.80, f32[4,256,32,64]{1,0,3,2:T(4,128)} %reshape.314, f32[4,256,32]{1,2,0:T(8,128)S(1)} %copy-done.36), kind=kOutput, calls=%fused_computation.114 | convolution fusion | flops 3226468352 | bytes 12189712 | tf_op jit(solution)/shard_map/transpose(jvp(btn,bhpn->bthp))/dot_general | solution.py:93
  465.8 2.4 convolution_add_fusion.2
  468.4 17.7 %fusion.78 = f32[4,256,128]{2,1,0:T(8,128)S(1)} fusion(f32[1,32,64,128]{3,2,1,0:T(8,128)} %copy-done.26, f32[1,32,64,128]{3,2,1,0:T(8,128)} %get-tuple-element.50, f32[1,32,64,128]{3,2,1,0:T(8,128)} %get-tuple-element.66, f32[4,256,32,64]{1,0,3,2:T(4,128)} %reshape.306, f32[4,256,32]{1,2,0:T(8,128)S(1)} %copy-done.33), kind=kOutput, calls=%fused_computation.113 | convolution fusion | flops 3225419776 | bytes 12189696 | tf_op jit(solution)/shard_map/transpose(jvp(bshp,bsn->bhpn))/dot_general | solution.py:82
  486.2 1.9 convolution_add_fusion.1
  488.3 33.8 %bitcast_add_fusion = f32[4,256,32,64]{1,3,2,0:T(8,128)} fusion(f32[4,256,32,64]{1,3,2,0:T(8,128)} %get-tuple-element.84, f32[4,256,32]{1,2,0:T(8,128)S(1)} %copy-done.33, f32[4,32,256]{2,1,0:T(8,128)S(1)} %bitcast.242, f32[4,256,256]{2,1,0:T(8,128)} %copy-done.30, f32[4,256,256]{2,1,0:T(8,128)} %and_convert_fusion, f32[4,32,256]{2,1,0:T(8,128)S(1)} %copy-done.39, ...), kind=kOutput, calls=%fused_computation.58 | convolution fusion | flops 6488588288 | bytes 27656192 | tf_op jit(solution)/shard_map/transpose(jvp(bhts,bshp->bthp))/dot_general | solution.py:72
  522.2 14.0 %copy.235 = f32[4,256,32,64]{1,0,3,2:T(4,128)} copy(f32[4,256,32,64]{1,3,2,0:T(8,128)} %bitcast_add_fusion) | data formatting | bytes 16777216 | tf_op jit(solution)/shard_map/transpose(jvp(bhts,bshp->bthp))/add_any | solution.py:72
  536.2 5.7 copy.266
  541.9 1.1 fusion.128
  543.1 4.1 multiply_add_fusion.1
  547.2 27.2 %fusion.126 = (f32[2304]{0:T(1024)S(1)}, f32[2304]{0:T(1024)S(1)}, f32[2304]{0:T(1024)S(1)}, f32[2304]{0:T(1024)S(1)}, f32[2304]{0:T(1024)S(1)}, /*index=5*/f32[1024,2304]{0,1:T(8,128)}) fusion(f32[1024,4384]{0,1:T(8,128)} %fusion.124, f32[1024]{0:T(1024)S(1)} %copy-done.63, f32[1024,2304]{0,1:T(8,128)} %copy-done.1, f32[1024]{0:T(1024)S(1)} %copy-done.61, ...), kind=kLoop, calls=%fused_computation.223 | loop fusion | flops 54252288 | bytes 47244288 | tf_op jit(solution)/shard_map/transpose(jvp())/reduce_sum | solution.py:42
  574.5 13.9 %multiply_multiply_fusion = (f32[1024,2304]{0,1:T(8,128)S(1)}, f32[1024,2304]{0,1:T(8,128)}, f32[1024,2304]{0,1:T(8,128)}) fusion(f32[1024,2304]{0,1:T(8,128)} %get-tuple-element.48, f32[2304]{0:T(1024)S(1)} %copy-done.53, f32[1024]{0:T(1024)S(1)} %copy-done.61, f32[1024]{0:T(1024)S(1)} %copy-done.63, f32[2304]{0:T(1024)S(1)} %copy-done.51, ...), kind=kLoop, calls=%fused_computation.49 | loop fusion | flops 14155776 | bytes 37788672 | tf_op jit(solution)/shard_map/transpose(jvp())/mul | solution.py:47
  588.4 14.7 %fusion.31 = f32[1024,2304]{0,1:T(8,128)} fusion(f32[1024,2304]{0,1:T(8,128)} %get-tuple-element.63, f32[1024,2304]{0,1:T(8,128)} %get-tuple-element.62, f32[1024,2304]{0,1:T(8,128)S(1)} %get-tuple-element.61, f32[1024,2304]{0,1:T(8,128)S(1)} %copy-done, f32[2304]{0:T(1024)S(1)} %copy-done.47), kind=kLoop, calls=%fused_computation.42 | loop fusion | flops 9437184 | bytes 47195136 | tf_op jit(solution)/shard_map/transpose(jvp())/add_any | solution.py:42
  603.1 19.8 %fusion.123 = f32[1024,4384]{1,0:T(8,128)} fusion(f32[1024,1024]{1,0:T(8,128)} %param.12, f32[1024]{0:T(1024)S(1)} %copy-done.74, f32[1024]{0:T(1024)S(1)} %copy-done.76, f32[1024,2048]{0,1:T(8,128)} %get-tuple-element.60, f32[1024,2304]{0,1:T(8,128)} %fusion.31, f32[1024,32]{0,1:T(8,128)S(1)} %get-tuple-element.47), kind=kOutput, calls=%fused_computation.220 | convolution fusion | flops 9210527744 | bytes 40116224 | tf_op jit(solution)/shard_map/dot_general | solution.py:26
  623.0 0.6 copy-done.70
  623.9 19.8 %multiply_reduce_fusion.10 = (f32[1024]{0:T(1024)S(1)}, f32[1024]{0:T(1024)S(1)}, f32[1024,1024]{1,0:T(8,128)}) fusion(f32[1024,1024]{1,0:T(8,128)} %param.12, f32[1024]{0:T(1024)S(1)} %copy-done.76, f32[1024]{0:T(1024)S(1)} %copy-done.74, bf16[1024,4384]{1,0:T(8,128)(2,1)} %all-gather.4.cloned.1.call-done, f32[1024,2048]{0,1:T(8,128)} %get-tuple-element.60, ...), kind=kOutput, calls=%fused_computation.96 | convolution fusion | flops 9213671424 | bytes 35340288 | tf_op jit(solution)/shard_map/dot_general | solution.py:26
  643.7 40.6 %all-reduce.33 = (f32[1024]{0:T(1024)S(1)}, f32[2304,4]{0,1:T(4,128)S(1)}, f32[2304]{0:T(1024)S(1)}, f32[32]{0:T(128)}, f32[32]{0:T(128)}, /*index=5*/f32[32]{0:T(128)}, f32[2048]{0:T(1024)S(1)}) all-reduce(f32[1024]{0:T(1024)S(1)} %get-tuple-element.27, ...), channel_id=2, replica_groups=mesh['dp'=16,'fsdp'=2] {'dp','fsdp'}, use_global_device_ids=true, to_apply=%region_21.22.clone | all-reduce | flops 14688 | bytes 117504
  684.8 0.6 dynamic-slice.2
  686.0 0.6 constant_dynamic-slice_fusion
  686.7 7.4 fusion.60
  694.1 1.3 copy-done.90
  695.4 9.8 convolution_add_fusion
  705.2 305.2 %reduce-scatter.4.cloned.1.call-done = f32[32,4384]{1,0:T(8,128)} async-done(((f32[1024,4384]{1,0:T(8,128)}), f32[32,4384]{1,0:T(8,128)}) %reduce-scatter.4.cloned.1.call-update) | async-done | bytes 561168 | tf_op jit(solution)/shard_map/reduce_scatter | solution.py:164
  (284 shorter events, 8.2 us)
Async XLA Ops:
  7.2 124.9 %all-gather.4.cloned.1.call-start = ((), (), s32[]{:S(2)}) async-start(), calls=%async_computation.2 | async-start | bytes 9461760 | tf_op jit(solution)/shard_map/all_gather | solution.py:118
  9.0 283.1 %all-gather.6.cloned.1.call-start = ((), (), s32[]{:S(2)}) async-start(), calls=%async_computation.3 | async-start | bytes 4325376 | tf_op jit(solution)/shard_map/all_gather | solution.py:122
  10.7 694.4 %reduce-scatter.6.cloned.1.call-start = ((), (), s32[]{:S(2)}) async-start(), calls=%async_computation.5 | async-start | bytes 8650752 | tf_op jit(solution)/shard_map/reduce_scatter | solution.py:168
  12.2 142.6 %copy-start.60 = (f32[1024]{0:T(1024)}, f32[1024]{0:T(1024)S(1)}, u32[]{:S(2)}) copy-start(f32[1024]{0:T(1024)S(1)} %get-tuple-element.76) | copy-start | bytes 12292
  12.2 142.6 %copy-start.62 = (f32[1024]{0:T(1024)}, f32[1024]{0:T(1024)S(1)}, u32[]{:S(2)}) copy-start(f32[1024]{0:T(1024)S(1)} %get-tuple-element.77) | copy-start | bytes 12292
  12.2 142.6 %copy-start.64 = (f32[1024]{0:T(1024)}, f32[1024]{0:T(1024)S(1)}, u32[]{:S(2)}) copy-start(f32[1024]{0:T(1024)S(1)} %get-tuple-element.78) | copy-start | bytes 12292
  58.0 92.0 %copy-start.73 = (f32[1024]{0:T(1024)}, f32[1024]{0:T(1024)S(1)}, u32[]{:S(2)}) copy-start(f32[1024]{0:T(1024)S(1)} %convert_element_type.95) | copy-start | bytes 12292
  60.5 89.4 %copy-start.75 = (f32[1024]{0:T(1024)}, f32[1024]{0:T(1024)S(1)}, u32[]{:S(2)}) copy-start(f32[1024]{0:T(1024)S(1)} %fusion.115) | copy-start | bytes 12292
  61.2 106.1 %copy-start.88 = (f32[32]{0:T(128)}, f32[32]{0:T(128)S(1)}, u32[]{:S(2)}) copy-start(f32[32]{0:T(128)S(1)} %exp.33) | copy-start | bytes 388
  129.0 25.8 %copy-start.46 = (f32[2304]{0:T(1024)}, f32[2304]{0:T(1024)S(1)}, u32[]{:S(2)}) copy-start(f32[2304]{0:T(1024)S(1)} %get-tuple-element.30) | copy-start | bytes 27652
  129.0 25.8 %copy-start.48 = (f32[2304]{0:T(1024)}, f32[2304]{0:T(1024)S(1)}, u32[]{:S(2)}) copy-start(f32[2304]{0:T(1024)S(1)} %get-tuple-element.31) | copy-start | bytes 27652
  129.0 25.8 %copy-start.50 = (f32[2304]{0:T(1024)}, f32[2304]{0:T(1024)S(1)}, u32[]{:S(2)}) copy-start(f32[2304]{0:T(1024)S(1)} %get-tuple-element.32) | copy-start | bytes 27652
  129.0 25.8 %copy-start.52 = (f32[2304]{0:T(1024)}, f32[2304]{0:T(1024)S(1)}, u32[]{:S(2)}) copy-start(f32[2304]{0:T(1024)S(1)} %get-tuple-element.33) | copy-start | bytes 27652
  131.7 270.5 %copy-start.71 = (f32[2048]{0:T(1024)}, f32[2048]{0:T(1024)S(1)}, u32[]{:S(2)}) copy-start(f32[2048]{0:T(1024)S(1)} %convert_element_type.109) | copy-start | bytes 24580
  131.8 61.5 %copy-start.58 = (f32[4,256]{1,0:T(4,128)}, f32[4,256]{1,0:T(4,128)S(1)}, u32[]{:S(2)}) copy-start(f32[4,256]{1,0:T(4,128)S(1)} %get-tuple-element.73) | copy-start | bytes 12292
  131.8 61.5 %copy-start.66 = (f32[4,256]{1,0:T(4,128)}, f32[4,256]{1,0:T(4,128)S(1)}, u32[]{:S(2)}) copy-start(f32[4,256]{1,0:T(4,128)S(1)} %get-tuple-element.72) | copy-start | bytes 12292
  132.0 61.2 %copy-start.82 = (f32[4]{0:T(128)}, f32[4]{0:T(128)S(1)}, u32[]{:S(2)}) copy-start(f32[4]{0:T(128)S(1)} %convert_reduce_fusion.1) | copy-start | bytes 52
  132.0 78.2 %copy-start.79 = (f32[4]{0:T(128)}, f32[4]{0:T(128)S(1)}, u32[]{:S(2)}) copy-start(f32[4]{0:T(128)S(1)} %pad.130.clone) | copy-start | bytes 52
  168.4 24.9 %copy-start.13 = (f32[1024,32]{0,1:T(8,128)}, f32[1024,32]{0,1:T(8,128)S(1)}, u32[]{:S(2)}) copy-start(f32[1024,32]{0,1:T(8,128)S(1)} %get-tuple-element.57) | copy-start | bytes 393220
  170.7 22.6 %copy-start.19 = (f32[4,32,2,128]{3,1,2,0:T(8,128)}, f32[4,32,2,128]{3,1,2,0:T(8,128)S(1)}, u32[]{:S(2)}) copy-start(f32[4,32,2,128]{3,1,2,0:T(8,128)S(1)} %reduce-window.19) | copy-start | bytes 393220
  171.0 22.4 %copy-start.54 = (f32[4,32,2]{1,2,0:T(2,128)}, f32[4,32,2]{1,2,0:T(2,128)S(1)}, u32[]{:S(2)}) copy-start(f32[4,32,2]{1,2,0:T(2,128)S(1)} %copy.205) | copy-start | bytes 3076
  191.9 16.2 %copy-start.17 = (f32[4,256,128]{2,1,0:T(8,128)}, f32[4,256,128]{2,1,0:T(8,128)S(1)}, u32[]{:S(2)}) copy-start(f32[4,256,128]{2,1,0:T(8,128)S(1)} %copy.208) | copy-start | bytes 1572868
  192.6 15.5 %copy-start.15 = (f32[4,256,128]{2,1,0:T(8,128)}, f32[4,256,128]{2,1,0:T(8,128)S(1)}, u32[]{:S(2)}) copy-start(f32[4,256,128]{2,1,0:T(8,128)S(1)} %copy.207) | copy-start | bytes 1572868
  192.9 17.4 %copy-start.11 = (f32[4,256,128,1]{2,1,3,0:T(8,128)}, f32[4,256,128,1]{2,1,3,0:T(8,128)S(1)}, u32[]{:S(2)}) copy-start(f32[4,256,128,1]{2,1,3,0:T(8,128)S(1)} %copy.238) | copy-start | bytes 1572868
  192.9 24.5 %copy-start.43 = (f32[4,4,8,256]{3,2,0,1:T(8,128)}, f32[4,4,8,256]{3,2,0,1:T(8,128)S(1)}, u32[]{:S(2)}) copy-start(f32[4,4,8,256]{3,2,0,1:T(8,128)S(1)} %copy.334) | copy-start | bytes 393220
  193.0 24.4 %copy-start.37 = (f32[4,32,256]{2,1,0:T(8,128)}, f32[4,32,256]{2,1,0:T(8,128)S(1)}, u32[]{:S(2)}) copy-start(f32[4,32,256]{2,1,0:T(8,128)S(1)} %copy_bitcast_fusion) | copy-start | bytes 393220
  193.2 15.3 %copy-start.56 = (f32[4,32]{1,0:T(4,128)}, f32[4,32]{1,0:T(4,128)S(1)}, u32[]{:S(2)}) copy-start(f32[4,32]{1,0:T(4,128)S(1)} %slice_reduce_fusion) | copy-start | bytes 1540
  193.3 15.2 %copy-start.84 = (f32[32]{0:T(128)}, f32[32]{0:T(128)S(1)}, u32[]{:S(2)}) copy-start(f32[32]{0:T(128)S(1)} %get-tuple-element.79) | copy-start | bytes 388
  193.5 24.0 %copy-start.34 = (f32[4,256,32]{1,2,0:T(8,128)}, f32[4,256,32]{1,2,0:T(8,128)S(1)}, u32[]{:S(2)}) copy-start(f32[4,256,32]{1,2,0:T(8,128)S(1)} %get-tuple-element.70) | copy-start | bytes 393220
  194.5 23.0 %copy-start.30 = (f32[4,256,256]{2,1,0:T(8,128)}, f32[4,256,256]{2,1,0:T(8,128)S(1)}, u32[]{:S(2)}) copy-start(f32[4,256,256]{2,1,0:T(8,128)S(1)} %fusion.132) | copy-start | bytes 3145732
  261.3 19.8 %slice-start = ((s8[9437184]{0:T(1024)(128)(4,1)}), s8[4194304]{0:T(1024)(128)(4,1)S(1)}, s32[]{:S(2)}) async-start(s8[9437184]{0:T(1024)(128)(4,1)} %bitcast.214), calls=%async_computation.6 | async-start | bytes 8388608
  261.3 19.8 %slice-start.1 = ((s8[9437184]{0:T(1024)(128)(4,1)}), s8[1048576]{0:T(1024)(128)(4,1)S(1)}, s32[]{:S(2)}) async-start(s8[9437184]{0:T(1024)(128)(4,1)} %bitcast.214), calls=%async_computation.7 | async-start | bytes 2097152
  292.1 110.1 %copy-start.77 = (f32[1024]{0:T(1024)}, f32[1024]{0:T(1024)S(1)}, u32[]{:S(2)}) copy-start(f32[1024]{0:T(1024)S(1)} %fusion.116) | copy-start | bytes 12292
  319.8 24.1 %copy-start.29 = (f32[4,256,256]{2,1,0:T(8,128)S(1)}, f32[4,256,256]{2,1,0:T(8,128)}, u32[]{:S(2)}) copy-start(f32[4,256,256]{2,1,0:T(8,128)} %and_convert_fusion) | copy-start | bytes 3145732
  319.8 24.1 %copy-start.31 = (f32[4,256,256]{2,1,0:T(8,128)S(1)}, f32[4,256,256]{2,1,0:T(8,128)}, u32[]{:S(2)}) copy-start(f32[4,256,256]{2,1,0:T(8,128)} %copy-done.30) | copy-start | bytes 3145732
  330.5 71.8 %slice-start.7 = ((s8[8388608]{0:T(1024)(128)(4,1)}), s8[4194304]{0:T(1024)(128)(4,1)S(1)}, s32[]{:S(2)}) async-start(s8[8388608]{0:T(1024)(128)(4,1)} %bitcast.222), calls=%async_computation.13 | async-start | bytes 8388608
  343.9 58.3 %slice-start.8 = ((s8[8388608]{0:T(1024)(128)(4,1)}), s8[4194304]{0:T(1024)(128)(4,1)S(1)}, s32[]{:S(2)}) async-start(s8[8388608]{0:T(1024)(128)(4,1)} %bitcast.222), calls=%async_computation.14 | async-start | bytes 8388608
  343.9 58.3 %copy-start.27 = (f32[1024,1024]{1,0:T(8,128)S(1)}, f32[1024,1024]{1,0:T(8,128)}, u32[]{:S(2)}) copy-start(f32[1024,1024]{1,0:T(8,128)} %param.13) | copy-start | bytes 12582916
  412.7 15.0 %copy-start.26 = (f32[1,32,64,128]{3,2,1,0:T(8,128)}, f32[1,32,64,128]{3,2,1,0:T(8,128)S(1)}, u32[]{:S(2)}) copy-start(f32[1,32,64,128]{3,2,1,0:T(8,128)S(1)} %get-tuple-element.49) | copy-start | bytes 3145732
  412.8 597.6 %reduce-scatter.4.cloned.1.call-start = ((), (), s32[]{:S(2)}) async-start(), calls=%async_computation.4 | async-start | bytes 18923520 | tf_op jit(solution)/shard_map/reduce_scatter | solution.py:164
  412.8 14.9 %copy-start.14 = (f32[1024,32]{0,1:T(8,128)S(1)}, f32[1024,32]{0,1:T(8,128)}, u32[]{:S(2)}) copy-start(f32[1024,32]{0,1:T(8,128)} %copy-done.13) | copy-start | bytes 393220
  412.8 14.9 %copy-start.20 = (f32[4,32,2,128]{3,1,2,0:T(8,128)S(1)}, f32[4,32,2,128]{3,1,2,0:T(8,128)}, u32[]{:S(2)}) copy-start(f32[4,32,2,128]{3,1,2,0:T(8,128)} %copy-done.19) | copy-start | bytes 393220
  412.8 14.9 %copy-start.55 = (f32[4,32,2]{1,2,0:T(2,128)S(1)}, f32[4,32,2]{1,2,0:T(2,128)}, u32[]{:S(2)}) copy-start(f32[4,32,2]{1,2,0:T(2,128)} %copy-done.54) | copy-start | bytes 3076
  412.8 14.9 %copy-start.57 = (f32[4,32]{1,0:T(4,128)S(1)}, f32[4,32]{1,0:T(4,128)}, u32[]{:S(2)}) copy-start(f32[4,32]{1,0:T(4,128)} %copy-done.56) | copy-start | bytes 1540
  412.9 14.9 %copy-start.59 = (f32[4,256]{1,0:T(4,128)S(1)}, f32[4,256]{1,0:T(4,128)}, u32[]{:S(2)}) copy-start(f32[4,256]{1,0:T(4,128)} %copy-done.58) | copy-start | bytes 12292
  412.9 15.1 %copy-start.7 = (f32[4,32,64,128]{3,2,1,0:T(8,128)S(1)}, f32[4,32,64,128]{3,2,1,0:T(8,128)}, u32[]{:S(2)}) copy-start(f32[4,32,64,128]{3,2,1,0:T(8,128)} %fusion.44) | copy-start | bytes 12582916
  412.9 15.1 %copy-start.9 = (f32[4,32,64,128]{3,2,1,0:T(8,128)S(1)}, f32[4,32,64,128]{3,2,1,0:T(8,128)}, u32[]{:S(2)}) copy-start(f32[4,32,64,128]{3,2,1,0:T(8,128)} %copy-done.8) | copy-start | bytes 12582916
  412.9 15.1 %copy-start.85 = (f32[32]{0:T(128)S(1)}, f32[32]{0:T(128)}, u32[]{:S(2)}) copy-start(f32[32]{0:T(128)} %copy-done.84) | copy-start | bytes 388
  412.9 16.1 %copy-start.83 = (f32[4]{0:T(128)S(1)}, f32[4]{0:T(128)}, u32[]{:S(2)}) copy-start(f32[4]{0:T(128)} %copy-done.82) | copy-start | bytes 52
  429.2 19.2 %copy-start.22 = (f32[1,32,64,128]{3,2,1,0:T(8,128)S(1)}, f32[1,32,64,128]{3,2,1,0:T(8,128)}, u32[]{:S(2)}) copy-start(f32[1,32,64,128]{3,2,1,0:T(8,128)} %copy-done.21) | copy-start | bytes 3145732
  429.2 19.2 %copy-start.36 = (f32[4,256,32]{1,2,0:T(8,128)S(1)}, f32[4,256,32]{1,2,0:T(8,128)}, u32[]{:S(2)}) copy-start(f32[4,256,32]{1,2,0:T(8,128)} %copy-done.34) | copy-start | bytes 393220
  429.2 19.2 %copy-start.80 = (f32[4]{0:T(128)S(1)}, f32[4]{0:T(128)}, u32[]{:S(2)}) copy-start(f32[4]{0:T(128)} %copy-done.79) | copy-start | bytes 52
  437.9 27.9 %copy-start.18 = (f32[4,256,128]{2,1,0:T(8,128)S(1)}, f32[4,256,128]{2,1,0:T(8,128)}, u32[]{:S(2)}) copy-start(f32[4,256,128]{2,1,0:T(8,128)} %copy-done.17) | copy-start | bytes 1572868
  448.4 20.0 %copy-start.33 = (f32[4,256,32]{1,2,0:T(8,128)S(1)}, f32[4,256,32]{1,2,0:T(8,128)}, u32[]{:S(2)}) copy-start(f32[4,256,32]{1,2,0:T(8,128)} %copy-done.32) | copy-start | bytes 393220
  465.7 20.4 %copy-start.16 = (f32[4,256,128]{2,1,0:T(8,128)S(1)}, f32[4,256,128]{2,1,0:T(8,128)}, u32[]{:S(2)}) copy-start(f32[4,256,128]{2,1,0:T(8,128)} %copy-done.15) | copy-start | bytes 1572868
  465.7 20.4 %copy-start.25 = (f32[4,256,256]{2,1,0:T(8,128)S(1)}, f32[4,256,256]{2,1,0:T(8,128)}, u32[]{:S(2)}) copy-start(f32[4,256,256]{2,1,0:T(8,128)} %get-tuple-element.14) | copy-start | bytes 3145732
  468.4 19.9 %copy-start.39 = (f32[4,32,256]{2,1,0:T(8,128)S(1)}, f32[4,32,256]{2,1,0:T(8,128)}, u32[]{:S(2)}) copy-start(f32[4,32,256]{2,1,0:T(8,128)} %copy-done.37) | copy-start | bytes 393220
  468.4 19.9 %copy-start.45 = (f32[4,4,8,256]{3,2,0,1:T(8,128)S(1)}, f32[4,4,8,256]{3,2,0,1:T(8,128)}, u32[]{:S(2)}) copy-start(f32[4,4,8,256]{3,2,0,1:T(8,128)} %copy-done.43) | copy-start | bytes 393220
  522.2 20.9 %slice-start.3 = ((s8[8388608]{0:T(1024)(128)(4,1)}), s8[4194304]{0:T(1024)(128)(4,1)S(1)}, s32[]{:S(2)}) async-start(s8[8388608]{0:T(1024)(128)(4,1)} %bitcast.216), calls=%async_computation.9 | async-start | bytes 8388608
  547.2 27.3 %copy-start.49 = (f32[2304]{0:T(1024)S(1)}, f32[2304]{0:T(1024)}, u32[]{:S(2)}) copy-start(f32[2304]{0:T(1024)} %copy-done.48) | copy-start | bytes 27652
  547.2 27.3 %copy-start.51 = (f32[2304]{0:T(1024)S(1)}, f32[2304]{0:T(1024)}, u32[]{:S(2)}) copy-start(f32[2304]{0:T(1024)} %copy-done.50) | copy-start | bytes 27652
  547.2 27.3 %copy-start.53 = (f32[2304]{0:T(1024)S(1)}, f32[2304]{0:T(1024)}, u32[]{:S(2)}) copy-start(f32[2304]{0:T(1024)} %copy-done.52) | copy-start | bytes 27652
  623.8 19.8 %copy-start.81 = (f32[2048]{0:T(1024)S(1)}, f32[2048]{0:T(1024)}, u32[]{:S(2)}) copy-start(f32[2048]{0:T(1024)} %get-tuple-element.18) | copy-start | bytes 24580
  623.9 62.8 %copy-start.69 = (f32[1024]{0:T(1024)S(1)}, f32[1024]{0:T(1024)}, u32[]{:S(2)}) copy-start(f32[1024]{0:T(1024)} %copy-done.68) | copy-start | bytes 12292
  (41 other events, 367.3 us)
Sparse Core Ops, SparseCore 0:
  11.4 83.6 all-gather.3
  98.6 60.8 all-gather.5
  412.9 178.9 reduce-scatter.5
  623.0 387.2 reduce-scatter.3
where the time goes:
time: 1020 us
  matrix products  308 us (30%)
  waiting for transfers between devices  305 us (30%)
  blocking collectives  150 us (15%)
  other arithmetic  147 us (14%)
  local copies, waits for them, and re-layouts  90.8 us (9%)
  between operations  15.7 us (2%)
    reduce_scatter x1, waiting for transfers between devices, local(): lax.psum_scatter(terms[1], ('dp', 'fsdp'), scatter_dimension=0, tiled=True)  305 us
    dot_general x3, matrix products, mixer(): jnp.einsum('bhts,bshp->bthp', scores, block_values, precision=highest)  133 us
    unnamed x2, blocking collectives  83.1 us
    all_gather x1, blocking collectives, local(): lax.all_gather(conv_weight.astype(jnp.bfloat16), ('dp', 'fsdp'), axis=0,...  66.8 us
    dot_general x4, matrix products, contract(): lax.dot_general(left, right, (((left_dim,), (right_dim,)), ((), ())), pre...  58.9 us
    dot_general x3, matrix products, mixer(): jnp.einsum('bshp,bsn->bhpn', weighted_values, block_b, precision=highest)  46.1 us
    dot_general x3, matrix products, mixer(): jnp.einsum('btn,bhpn->bthp', block_c, start_states, precision=highest)  37.9 us
    reduce_sum x1, other arithmetic, mixer(): conv_sum = conv_bias + conv_in * conv_weight[:, kernel - 1]  27.2 us
  transfers between devices with their start and end apart: 4, of which 1 were waited for; matrix products, arithmetic and copies ran while one was open for 41% of the time, Pallas kernels for 0%

commit v1 on v0

v1 whole, which is shorter than its diff:
```python
import functools

import jax
import jax.numpy as jnp
from jax import lax
from jax.experimental import pallas as pl
from jax.experimental.pallas import tpu as pltpu
from jax.sharding import PartitionSpec as P

AXES = ("chip", "core", "fsdp")
CHIPS = ("chip", "fsdp")
SHARDS = 32
PIECES = tuple(c | y | x for c in (0, 2) for y in (0, 1) for x in (0, 4))
BLOCK = 128
GROUP = 256
EPS = 1e-05
LOG2E = 1.4426950408889634
VMEM_LIMIT = 60 * 1024 * 1024
f32 = jnp.float32
bf16 = jnp.bfloat16
highest = lax.Precision.HIGHEST


def dot(a, b):
    return jnp.dot(a, b, preferred_element_type=f32)


def dot_nt(a, b):
    return lax.dot_general(a, b, (((1,), (1,)), ((), ())), preferred_element_type=f32)


def dot_tn(a, b):
    return lax.dot_general(a, b, (((0,), (0,)), ((), ())), preferred_element_type=f32)


def sigmoid(v):
    return 0.5 * jnp.tanh(0.5 * v) + 0.5


def iota(shape, axis):
    return lax.broadcasted_iota(jnp.int32, shape, axis)


def rows8(v):
    return jnp.sum(v.reshape(v.shape[0] // 8, 8, v.shape[1]), axis=0)


def scene_of(place, sm):
    scene = jnp.zeros(place.shape, jnp.int32)
    for i in range(3):
        scene = scene + jnp.where(place >= sm[i], 1, 0)
    return scene


def call(kernel, out, grid=None, in_specs=None, out_specs=None, scratch=(), name=None, flops=0, size=0):
    return pl.pallas_call(
        kernel,
        out_shape=out,
        grid=grid or (1,),
        in_specs=in_specs,
        out_specs=out_specs,
        scratch_shapes=scratch,
        name=name,
        compiler_params=pltpu.CompilerParams(
            vmem_limit_bytes=VMEM_LIMIT, dimension_semantics=("arbitrary",)
        ),
        cost_estimate=pl.CostEstimate(flops=int(flops), bytes_accessed=int(size), transcendentals=0),
    )


def whole(shape):
    return pl.BlockSpec(shape, lambda g: (0,) * len(shape))


SMEM = pl.BlockSpec(memory_space=pltpu.SMEM)


def struct(shape, dtype=f32):
    return jax.ShapeDtypeStruct(shape, dtype)


def conv_block(window, masks, taps, width):
    current = window[8:]
    total = taps[4:5] + current * taps[3:4]
    shifted = [current]
    for off in range(1, width):
        moved = window[8 - off : 8 - off + BLOCK] * masks[:, off - 1 : off]
        shifted.append(moved)
        total = total + moved * taps[width - 1 - off : width - off]
    return total, shifted


def conv_back(window, masks, taps, width):
    total = window[:BLOCK] * taps[width - 1 : width]
    for off in range(1, width):
        moved = pltpu.roll(window * masks[:, off - 1 : off], window.shape[0] - off, 0)[:BLOCK]
        total = total + moved * taps[width - 1 - off : width - off]
    return total


def unpack_kernel(sm, *refs):
    pieces, (skip_ref, w_ref, taps_ref, gain_ref) = refs[: len(PIECES)], refs[len(PIECES) :]
    assemble(sm, pieces, w_ref, 32)
    row, col = iota((8 * SHARDS, 32 * SHARDS), 0), iota((8 * SHARDS, 32 * SHARDS), 1)
    pick = jnp.where(col == (row & (SHARDS - 1)) * 32 + row // SHARDS, 1.0, 0.0).astype(bf16)
    packed = dot(pick, w_ref[:, 256:384]).astype(bf16)

    def spread(kind, lane, size):
        total = size * SHARDS
        place = iota((1, total), 1)
        owner, within = place // size, place % size
        copy = jnp.where(iota((128, total), 0) == within + lane, 1.0, 0.0).astype(bf16)
        values = dot(packed[kind * SHARDS : (kind + 1) * SHARDS, :], copy)
        return jnp.sum(jnp.where(iota((SHARDS, total), 0) == owner, values, 0.0), axis=0, keepdims=True)

    taps_ref[...] = jnp.zeros(taps_ref.shape, f32)
    gain_ref[...] = jnp.broadcast_to(spread(0, 32, 32), gain_ref.shape)
    inner = skip_ref.shape[1]
    taps_ref[6:7, :inner] = spread(0, 64, inner // SHARDS)
    channels = taps_ref.shape[1]
    for k in range(5):
        taps_ref[k : k + 1, :] = spread(k + 1, 32, channels // SHARDS)
    taps_ref[5:6, :inner] = skip_ref[0:1, :]


def unpack(sm, pieces, skip, channels, width):
    outs = [struct((width, 384), bf16), struct((8, channels)), struct((8, width))]
    return call(
        unpack_kernel,
        outs,
        in_specs=[SMEM] + [whole(a.shape) for a in (*pieces, skip)],
        out_specs=[whole(o.shape) for o in outs],
        name="unpack",
        size=2e6,
    )(sm, *pieces, skip)


def core_first(shard):
    return (shard >> 1 & 1) * 16 + (shard >> 2) * 2 + (shard & 1)


def prep_kernel(
    ring, sm, x_ref, gain_ref, w_ref, taps_ref, head_ref,
    normed_ref, normt_ref, cin_ref, b_ref, c_ref, bt_ref, ct_ref, s_ref, st_ref,
    cum_ref, cumt_ref, ea_ref, eb_ref, step_ref, mask_ref, cs_scr,
):
    tokens = x_ref.shape[0]
    x = x_ref[...]
    scale = lax.rsqrt(jnp.mean(x * x, axis=-1, keepdims=True) + EPS)
    normed_low = (x * scale * gain_ref[0:1, :]).astype(bf16)
    normed_ref[...] = normed_low
    flipped = normed_low.astype(f32).T.astype(bf16)
    if ring:
        for shard in range(SHARDS):
            at = core_first(shard) * 32
            normt_ref[at : at + 32, :] = flipped[shard * 32 : shard * 32 + 32, :]
    else:
        normt_ref[...] = flipped
    proj = dot(normed_low, w_ref[...])
    lanes = iota((1, 128), 1)
    heads = cumt_ref.shape[0]
    is_head = lanes < heads
    cin_low = proj[:, :256].astype(bf16)
    cin_ref[...] = cin_low
    cs_scr[0:8, :] = jnp.zeros((8, 256), f32)
    cs_scr[pl.ds(8, tokens), :] = cin_low.astype(f32)
    step_ref[...] = jnp.where(is_head, proj[:, 256:384] + head_ref[0:1, :], 0.0)
    taps = taps_ref[...]

    def block(k, _):
        t0 = pl.multiple_of(k * BLOCK, BLOCK)
        rows = pl.ds(t0, BLOCK)
        place = iota((BLOCK, 128), 0) + t0
        lane = iota((BLOCK, 128), 1)
        scene = scene_of(place, sm)
        before = place - lane - 1
        same = (before >= 0) & (scene_of(before, sm) == scene)
        mask = jnp.where(lane < 3, jnp.where(same, 1.0, 0.0), jnp.where(place < sm[2], 1.0, 0.0))
        mask_ref[rows, :] = mask
        conv, _ = conv_block(cs_scr[pl.ds(t0, BLOCK + 8), :], mask, taps, 4)
        act = conv * sigmoid(conv)
        b_low = act[:, :128].astype(bf16)
        c_low = act[:, 128:].astype(bf16)
        b_ref[rows, :] = b_low
        c_ref[rows, :] = c_low
        bt_ref[:, rows] = act[:, :128].T.astype(bf16)
        ct_ref[:, rows] = act[:, 128:].T.astype(bf16)
        other = scene_of(lane + t0, sm)
        low = (lane + t0 <= place) & (other == scene)
        s_ref[rows, :] = jnp.where(low, dot_nt(c_low, b_low), 0.0)
        high = (lane + t0 >= place) & (other == scene)
        st_ref[rows, :] = jnp.where(high, dot_nt(b_low, c_low), 0.0)
        step = step_ref[rows, :]
        dt = jnp.maximum(step, 0.0) + jnp.log1p(jnp.exp(-jnp.abs(step)))
        dt = jnp.where(is_head, dt, 0.0)
        log_decay = dt * (head_ref[1:2, :] * -LOG2E)
        lower = jnp.where(lane <= iota((BLOCK, 128), 0), 1.0, 0.0)
        cum = jnp.dot(lower, log_decay, precision=highest, preferred_element_type=f32)
        cum_ref[rows, :] = cum
        cumt_ref[:, rows] = cum.T[:heads, :]
        first = jnp.full((1, 128), t0 - 1, jnp.int32)
        last = jnp.full((1, 128), t0 + BLOCK - 1, jnp.int32)
        entering = (scene_of(first, sm) == scene) & (first >= 0) & is_head
        final = (scene_of(last, sm) == scene) & is_head
        grow = jnp.where(entering, jnp.exp2(cum), 0.0)
        end = jnp.where(final, jnp.exp2(cum[BLOCK - 1 :] - cum), 0.0)

        def packed(v):
            hi = v.astype(bf16).astype(f32)
            return hi + pltpu.roll((v - hi).astype(bf16).astype(f32), 32, 1)

        ea_ref[rows, :] = (packed(dt) + pltpu.roll(packed(grow), 64, 1)).astype(bf16)
        eb_ref[rows, :] = packed(end).astype(bf16)
        return 0

    mask_ref[pl.ds(tokens, 8), :] = jnp.zeros((8, 128), f32)
    lax.fori_loop(0, tokens // BLOCK, block, 0)


def prep(ring, sm, x, gain, w_bc, taps, head, heads):
    tokens, width = x.shape
    wide = (tokens, 128)
    outs = [
        struct(x.shape, bf16), struct((width, tokens), bf16), struct((tokens, 256), bf16),
        struct(wide, bf16), struct(wide, bf16), struct((128, tokens), bf16), struct((128, tokens), bf16),
        struct(wide), struct(wide), struct(wide), struct((heads, tokens)), struct(wide, bf16), struct(wide, bf16),
        struct(wide), struct((tokens + 8, 128)),
    ]
    args = (x, gain, w_bc, taps, head)
    return call(
        functools.partial(prep_kernel, ring),
        outs,
        in_specs=[SMEM] + [whole(a.shape) for a in args],
        out_specs=[whole(o.shape) for o in outs],
        scratch=[pltpu.VMEM((tokens + 8, 256), f32)],
        name="prep",
        flops=2 * tokens * width * 384,
        size=12e6,
    )(sm, *args)


def fill_spread(e_scr, group):
    row = iota((128, 768), 0)
    col = iota((128, 768), 1)
    head = 4 * group + (col % GROUP) // 64
    part = jnp.where(col < GROUP, 0, jnp.where(col < 2 * GROUP, 64, 0))
    hit = (row == head + part) | (row == head + part + 32)
    e_scr[...] = jnp.where(hit, 1.0, 0.0).astype(bf16)


def pair_masks():
    low = jnp.where(iota((1, 128), 1) < 64, 1.0, 0.0).astype(bf16)
    high = jnp.where(iota((1, 128), 1) < 64, 0.0, 1.0).astype(bf16)
    return low, high


def assemble(sm, pieces, out_ref, block):
    for i, piece in enumerate(pieces):
        for j in range(4):
            shard = sm[3] ^ (PIECES[i] | j << 3)
            out_ref[pl.ds(pl.multiple_of(shard * block, block), block), :] = piece[j * block : (j + 1) * block, :]


def fwd_kernel(*refs):
    base, ring, sm = refs[:3]
    if ring:
        n = len(PIECES)
        gates, values = refs[3 : 3 + n], refs[3 + n : 3 + 2 * n]
        rest = list(refs[3 + 2 * n :])
        wv_ref, wg_ref = rest.pop(15), rest.pop(14)
        assemble(sm, gates, wg_ref, 32)
        assemble(sm, values, wv_ref, 32)
        rest[1:1] = [wg_ref, wv_ref]
    else:
        rest = list(refs[5:])
        rest[1:1] = refs[3:5]
    fwd_body(base, *rest)


def fwd_body(
    base, normed_ref, wg_ref, wv_ref, taps_ref, ea_ref, eb_ref, cum_ref, cumt_ref, c_ref, bt_ref, s_ref, mask_ref,
    z_ref, cin_ref, y_ref, h_ref, cs_scr, e_scr, h_scr,
):
    group = pl.program_id(0) + base
    tokens = normed_ref.shape[0]
    normed = normed_ref[...]
    z_ref[...] = dot(normed, wg_ref[...]).astype(bf16)
    cin_low = dot(normed, wv_ref[...]).astype(bf16)
    cin_ref[...] = cin_low
    cs_scr[0:8, :] = jnp.zeros((8, GROUP), f32)
    cs_scr[pl.ds(8, tokens), :] = cin_low.astype(f32)
    fill_spread(e_scr, group)
    h_scr[...] = jnp.zeros(h_scr.shape, f32)
    taps = taps_ref[...]
    m_low, m_high = pair_masks()

    def block(k, _):
        t0 = pl.multiple_of(k * BLOCK, BLOCK)
        rows = pl.ds(t0, BLOCK)
        mask = mask_ref[rows, :]
        conv, _ = conv_block(cs_scr[pl.ds(t0, BLOCK + 8), :], mask, taps, 4)
        v = conv * sigmoid(conv)
        ea = dot(ea_ref[rows, :], e_scr[:, : 2 * GROUP])
        wx = dot(eb_ref[rows, :], e_scr[:, 2 * GROUP :])
        dtx, ex = ea[:, :GROUP], ea[:, GROUP:]
        vd_low = (v * dtx).astype(bf16)
        h_old = h_scr[...]
        h_low = h_old.astype(bf16)
        h_ref[rows, :] = h_low
        carried = dot(c_ref[rows, :], h_low) * ex
        cums = pltpu.roll(cum_ref[rows, :], 128 - 4 * group, 1)
        s = s_ref[rows, :]
        inside = []
        for pair in range(2):
            weights = []
            for j in (2 * pair, 2 * pair + 1):
                spread = cums[:, j : j + 1] - cumt_ref[0, j : j + 1, rows]
                weights.append((jnp.exp2(jnp.minimum(spread, 0.0)) * s).astype(bf16))
            vp = vd_low[:, pair * 128 : pair * 128 + 128]
            stack = jnp.concatenate([vp * m_low, vp * m_high], axis=0)
            inside.append(dot(jnp.concatenate(weights, axis=1), stack))
        y_ref[rows, :] = jnp.concatenate(inside, axis=1) + carried + taps[5:6] * v
        fresh = dot(bt_ref[:, rows], (vd_low.astype(f32) * wx).astype(bf16))
        h_scr[...] = h_old * ex[BLOCK - 1 :] + fresh
        return 0

    lax.fori_loop(0, tokens // BLOCK, block, 0)


def fwd(base, count, ring, sm, normed, gates, values, inner, taps, pre):
    tokens, width = normed.shape
    full = lambda a: whole(a.shape)
    ea, eb, cum, cumt, c, bt, s, mask = pre
    first = inner // GROUP
    col = lambda rows, dtype: struct((rows, count * GROUP), dtype)
    block = lambda rows: pl.BlockSpec((rows, GROUP), lambda g: (0, g))
    outs = [col(tokens, bf16), col(tokens, bf16), col(tokens, f32), col(tokens, bf16)]
    if ring:
        w_specs = [block(a.shape[0]) for a in (*gates, *values)]
        outs += [col(width, bf16)] * 2
    else:
        w_specs = [
            pl.BlockSpec((width, GROUP), lambda g: (0, base + g)),
            pl.BlockSpec((width, GROUP), lambda g: (0, first + base + g)),
        ]
    return call(
        functools.partial(fwd_kernel, base, ring),
        outs,
        grid=(count,),
        in_specs=[SMEM] + w_specs + [
            full(normed),
            pl.BlockSpec((8, GROUP), lambda g: (0, base + g)),
            full(ea), full(eb), full(cum),
            pl.BlockSpec((1, 4, tokens), lambda g: (base + g, 0, 0)),
            full(c), full(bt), full(s), full(mask),
        ],
        out_specs=[block(o.shape[0]) for o in outs],
        scratch=[pltpu.VMEM((tokens + 8, GROUP), f32), pltpu.VMEM((128, 3 * GROUP), bf16), pltpu.VMEM((128, GROUP), f32)],
        name=f"fwd{base}",
        flops=count * 2 * tokens * width * 2 * GROUP * 3,
        size=count * 4e6,
    )(sm, *gates, *values, normed, taps, ea, eb, cum, cumt, c, bt, s, mask)


MID = 256
MID_C = 512


def mid_kernel(ring, chunks, sm, cot_ref, w_ref, taps_ref, mask_ref, *refs):
    zs, ys = refs[:chunks], refs[chunks : 2 * chunks]
    mixed_ref, dz_ref, dy_ref, gg_ref, *terms = refs[2 * chunks : -3]
    g_scr, u_scr, acc_scr = refs[-3:]
    step = pl.program_id(0)
    inner = dz_ref.shape[1]
    wide = inner // chunks
    alive = mask_ref[:, 3:4]
    cot_low = cot_ref[...].astype(bf16)
    square = jnp.zeros((MID, 128), f32)
    parts = [slice(i, i + MID_C) for i in range(0, inner, MID_C)]
    here = [(zs[p.start // wide], ys[p.start // wide], slice(p.start % wide, p.start % wide + MID_C)) for p in parts]
    for part, (z_ref, y_ref, cut) in zip(parts, here):
        z = z_ref[:, cut].astype(f32)
        g = y_ref[:, cut] * (z * sigmoid(z)) * alive
        g_scr[:, part] = g
        sq = g * g
        for i in range(0, MID_C, 128):
            square = square + sq[:, i : i + 128]
    r = lax.rsqrt(jnp.sum(square, axis=-1, keepdims=True) * (1.0 / inner) + EPS)
    cross = jnp.zeros((MID, 128), f32)
    for part in parts:
        gain = taps_ref[6:7, part]
        dm = dot_nt(cot_low, w_ref[part, :])
        g = g_scr[:, part]
        u = dm * gain
        u_scr[:, part] = u
        ug = u * g
        for i in range(0, MID_C, 128):
            cross = cross + ug[:, i : i + 128]
        gr = g * r
        mixed_ref[:, part] = (gr * gain).astype(bf16)
        gg = rows8(dm * gr)

        @pl.when(step == 0)
        def _():
            gg_ref[:, part] = gg

        @pl.when(step > 0)
        def _():
            gg_ref[:, part] += gg

    r3 = r * r * r * (jnp.sum(cross, axis=-1, keepdims=True) * (1.0 / inner))
    for part in parts:
        term = dot_tn(mixed_ref[:, part], cot_low)

        @pl.when(step == 0)
        def _():
            acc_scr[part, :] = term

        @pl.when(step > 0)
        def _():
            acc_scr[part, :] += term

    for part, (z_ref, y_ref, cut) in zip(parts, here):
        z = z_ref[:, cut].astype(f32)
        sig = sigmoid(z)
        dg = (u_scr[:, part] * r - g_scr[:, part] * r3) * alive
        dy_ref[:, part] = (dg * (z * sig)).astype(bf16)
        dz_ref[:, part] = (dg * y_ref[:, cut] * (sig * (1.0 + z * (1.0 - sig)))).astype(bf16)

    @pl.when(step == pl.num_programs(0) - 1)
    def _():
        if not ring:
            terms[0][...] = acc_scr[...].astype(bf16)
            return
        width = acc_scr.shape[1]
        for shard in range(SHARDS):
            at = core_first(shard) % 16 * 32
            for half in range(2):
                value = acc_scr[shard * 64 + half * 32 : shard * 64 + half * 32 + 32, :].astype(bf16)

                def put(ref):
                    ref[at : at + 32, half * width : (half + 1) * width] = value

                mine = (sm[3] >> 1 & 1) == (shard >> 1 & 1)
                pl.when(mine)(functools.partial(put, terms[0]))
                pl.when(jnp.logical_not(mine))(functools.partial(put, terms[1]))


def mid(ring, sm, cot, w_out, taps, mask, zs, ys):
    tokens, width = cot.shape
    inner = w_out.shape[0]
    row = lambda n: pl.BlockSpec((MID, n), lambda g: (g, 0))
    wide = struct((tokens, inner), bf16)
    outs = [wide, wide, wide, struct((8, inner))]
    outs += [struct((inner // 4, 2 * width), bf16)] * 2 if ring else [struct(w_out.shape, bf16)]
    return call(
        functools.partial(mid_kernel, ring, len(zs)),
        outs,
        grid=(tokens // MID,),
        in_specs=[SMEM, row(width), whole(w_out.shape), whole(taps.shape), row(128)] + [row(a.shape[1]) for a in (*zs, *ys)],
        out_specs=[row(inner)] * 3 + [whole(o.shape) for o in outs[3:]],
        scratch=[pltpu.VMEM((MID, inner), f32), pltpu.VMEM((MID, inner), f32), pltpu.VMEM(w_out.shape, f32)],
        name="mid",
        flops=4 * tokens * width * inner,
        size=30e6,
    )(sm, cot, w_out, taps, mask, *zs, *ys)


def branch_kernel(x_ref, m_ref, w_ref, out_ref):
    out_ref[...] = x_ref[...] + dot(m_ref[...], w_ref[...])


def branch(x, mixed, w_out):
    tokens, width = x.shape
    row = lambda n: pl.BlockSpec((MID, n), lambda g: (g, 0))
    return call(
        branch_kernel,
        struct(x.shape),
        grid=(tokens // MID,),
        in_specs=[row(width), row(mixed.shape[1]), whole(w_out.shape)],
        out_specs=row(width),
        name="branch",
        flops=2 * tokens * width * mixed.shape[1],
        size=16e6,
    )(x, mixed, w_out)


def bwd_kernel(
    base, cin_ref, y_ref, dy_ref, taps_ref, ea_ref, eb_ref, cum_ref, cumt_ref, b_ref, c_ref, ct_ref, st_ref, mask_ref, h_ref,
    dcin_ref, grad_ref, dst_ref, db_ref, dc_ref, dcum_ref, ddt_ref, cs_scr, ds_scr, e_scr, et_scr, h_scr,
):
    group = pl.program_id(0) + base
    tokens = cin_ref.shape[0]
    cs_scr[0:8, :] = jnp.zeros((8, GROUP), f32)
    cs_scr[pl.ds(8, tokens), :] = cin_ref[...].astype(f32)
    ds_scr[...] = jnp.zeros(ds_scr.shape, f32)
    fill_spread(e_scr, group)
    row, col = iota((GROUP, 128), 0), iota((GROUP, 128), 1)
    et_scr[...] = jnp.where(col == 4 * group + row // 64, 1.0, 0.0).astype(bf16)
    h_scr[...] = jnp.zeros(h_scr.shape, f32)
    taps = taps_ref[...]
    m_low, m_high = pair_masks()
    grad_ref[...] = jnp.zeros(grad_ref.shape, f32)

    @pl.when(pl.program_id(0) == 0)
    def _():
        for ref in (dst_ref, db_ref, dc_ref, dcum_ref, ddt_ref):
            ref[...] = jnp.zeros(ref.shape, f32)

    def to_heads(v):
        hi = v.astype(bf16)
        lo = (v - hi.astype(f32)).astype(bf16)
        return dot(hi, et_scr[...]) + dot(lo, et_scr[...])

    blocks = tokens // BLOCK

    def block(step, _):
        k = blocks - 1 - step
        t0 = pl.multiple_of(k * BLOCK, BLOCK)
        rows = pl.ds(t0, BLOCK)
        mask = mask_ref[rows, :]
        conv, shifted = conv_block(cs_scr[pl.ds(t0, BLOCK + 8), :], mask, taps, 4)
        sig = sigmoid(conv)
        v = conv * sig
        ea = dot(ea_ref[rows, :], e_scr[:, : 2 * GROUP])
        wx = dot(eb_ref[rows, :], e_scr[:, 2 * GROUP :])
        dtx, ex = ea[:, :GROUP], ea[:, GROUP:]
        vd_low = (v * dtx).astype(bf16)
        vd = vd_low.astype(f32)
        dy_low = dy_ref[rows, :]
        dy = dy_low.astype(f32)
        skip = taps[5:6]
        dh_old = h_scr[...]
        dh_low = dh_old.astype(bf16)
        h_low = h_ref[rows, :]
        dye = (dy * ex).astype(bf16)
        dc_ref[rows, :] += dot_nt(dye, h_low)
        db_ref[rows, :] += dot_nt((vd * wx).astype(bf16), dh_low)
        dvd_end = dot(b_ref[rows, :], dh_low) * wx
        cums = pltpu.roll(cum_ref[rows, :], 128 - 4 * group, 1)
        st = st_ref[rows, :]
        inside = []
        dst = jnp.zeros((BLOCK, BLOCK), f32)
        for pair in range(2):
            cols = slice(pair * 128, pair * 128 + 128)
            decays, weights = [], []
            for j in (2 * pair, 2 * pair + 1):
                spread = cumt_ref[0, j : j + 1, rows] - cums[:, j : j + 1]
                decay = jnp.exp2(jnp.minimum(spread, 0.0))
                decays.append(decay)
                weights.append((decay * st).astype(bf16))
            dyp = dy_low[:, cols]
            stack = jnp.concatenate([dyp * m_low, dyp * m_high], axis=0)
            inside.append(dot(jnp.concatenate(weights, axis=1), stack))
            cross = dot_nt(vd_low[:, cols], stack)
            dst = dst + cross[:, :128] * decays[0] + cross[:, 128:] * decays[1]
        dst_ref[rows, :] += dst
        dvd = jnp.concatenate(inside, axis=1) + dvd_end
        through = ex[BLOCK - 1 :]
        last = jnp.sum(vd * dvd_end, axis=0, keepdims=True) + through * jnp.sum(
            dh_old * h_low.astype(f32), axis=0, keepdims=True
        )
        p = dy * (y_ref[rows, :] - skip * v) - vd * dvd
        p = p + jnp.where(iota((BLOCK, 1), 0) == BLOCK - 1, last, 0.0)
        dcum_ref[rows, :] += to_heads(p)
        ddt_ref[rows, :] += to_heads(dvd * v)
        h_scr[...] = dh_old * through + dot(ct_ref[:, rows], dye)
        dconv = (dvd * dtx + skip * dy) * (sig * (1.0 + conv * (1.0 - sig)))
        window = jnp.concatenate([dconv, ds_scr[...]], axis=0)
        ds_scr[...] = dconv[:8]
        grads = [jnp.sum(rows8(dconv * shifted[3 - i]), axis=0, keepdims=True) for i in range(4)]
        grads.append(jnp.sum(rows8(dconv), axis=0, keepdims=True))
        grads.append(jnp.sum(rows8(dy * v), axis=0, keepdims=True))
        grads.append(jnp.zeros((2, GROUP), f32))
        grad_ref[...] += jnp.concatenate(grads, axis=0)
        dcin_ref[rows, :] = conv_back(
            window, mask_ref[pl.ds(t0, BLOCK + 8), :], taps, 4
        ).astype(bf16)
        return 0

    lax.fori_loop(0, blocks, block, 0)


def bwd(base, count, cin, y, dy, taps, pre, h):
    tokens = cin.shape[0]
    full = lambda a: whole(a.shape)
    ea, eb, cum, cumt, b, c, ct, st, mask = pre
    local = lambda rows: pl.BlockSpec((rows, GROUP), lambda g: (0, g))
    global_ = lambda rows: pl.BlockSpec((rows, GROUP), lambda g: (0, base + g))
    wide = struct((tokens, 128))
    return call(
        functools.partial(bwd_kernel, base),
        [struct((tokens, count * GROUP), bf16), struct((8, count * GROUP))] + [wide] * 5,
        grid=(count,),
        in_specs=[
            local(tokens), local(tokens), global_(tokens), global_(8),
            full(ea), full(eb), full(cum),
            pl.BlockSpec((1, 4, tokens), lambda g: (base + g, 0, 0)),
            full(b), full(c), full(ct), full(st), full(mask), local(tokens),
        ],
        out_specs=[local(tokens), local(8)] + [whole(wide.shape)] * 5,
        scratch=[
            pltpu.VMEM((tokens + 8, GROUP), f32), pltpu.VMEM((8, GROUP), f32),
            pltpu.VMEM((128, 3 * GROUP), bf16), pltpu.VMEM((GROUP, 128), bf16), pltpu.VMEM((128, GROUP), f32),
        ],
        name=f"bwd{base}",
        flops=count * 2 * tokens * 128 * GROUP * 8,
        size=count * 4e6,
    )(cin, y, dy, taps, ea, eb, cum, cumt, b, c, ct, st, mask, h)


def tail_kernel(sm, cin_ref, taps_ref, head_ref, b_ref, c_ref, step_ref, mask_ref, *refs):
    dp_ref, grad_ref, stat_ref, cs_scr, ds_scr = refs[-5:]
    sums = refs[:-5]
    tokens = cin_ref.shape[0]
    cs_scr[0:8, :] = jnp.zeros((8, 256), f32)
    cs_scr[pl.ds(8, tokens), :] = cin_ref[...].astype(f32)
    ds_scr[...] = jnp.zeros(ds_scr.shape, f32)
    taps = taps_ref[...]
    grad_ref[...] = jnp.zeros(grad_ref.shape, f32)
    stat_ref[...] = jnp.zeros(stat_ref.shape, f32)
    blocks = tokens // BLOCK

    def block(step, _):
        k = blocks - 1 - step
        t0 = pl.multiple_of(k * BLOCK, BLOCK)
        rows = pl.ds(t0, BLOCK)
        row, lane = iota((BLOCK, 128), 0), iota((BLOCK, 128), 1)
        dst_sum, db_sum, dc_sum, dcum_sum, ddt_sum = [
            functools.reduce(jnp.add, [ref[rows, :] for ref in sums[i::5]]) for i in range(5)
        ]
        keep = (lane >= row) & (scene_of(lane + t0, sm) == scene_of(row + t0, sm))
        dst = jnp.where(keep, dst_sum, 0.0).astype(bf16)
        db = db_sum + dot(dst, c_ref[rows, :])
        dc = dc_sum + dot_tn(dst, b_ref[rows, :])
        conv, shifted = conv_block(cs_scr[pl.ds(t0, BLOCK + 8), :], mask_ref[rows, :], taps, 4)
        sig = sigmoid(conv)
        dconv = jnp.concatenate([db, dc], axis=1) * (sig * (1.0 + conv * (1.0 - sig)))
        window = jnp.concatenate([dconv, ds_scr[...]], axis=0)
        ds_scr[...] = dconv[:8]
        grads = [jnp.sum(rows8(dconv * shifted[3 - i]), axis=0, keepdims=True) for i in range(4)]
        grads.append(jnp.sum(rows8(dconv), axis=0, keepdims=True))
        grads.append(jnp.zeros((3, 256), f32))
        grad_ref[...] += jnp.concatenate(grads, axis=0)
        dcin = conv_back(window, mask_ref[pl.ds(t0, BLOCK + 8), :], taps, 4)
        upper = jnp.where(lane >= row, 1.0, 0.0)
        dlog = jnp.dot(upper, dcum_sum, precision=highest, preferred_element_type=f32)
        step_in = step_ref[rows, :]
        dt = jnp.maximum(step_in, 0.0) + jnp.log1p(jnp.exp(-jnp.abs(step_in)))
        rate = head_ref[1:2, :]
        dstep = (ddt_sum - dlog * rate) * sigmoid(step_in)
        dalog = -dlog * dt * rate
        stat_ref[...] += jnp.concatenate(
            [
                jnp.sum(rows8(dstep), axis=0, keepdims=True),
                jnp.sum(rows8(dalog), axis=0, keepdims=True),
                jnp.zeros((6, 128), f32),
            ],
            axis=0,
        )
        dp_ref[rows, :] = jnp.concatenate([dcin, dstep], axis=1).astype(bf16)
        return 0

    lax.fori_loop(0, blocks, block, 0)


def tail(sm, cin, taps, head, b, c, step, mask, sums):
    tokens = cin.shape[0]
    args = (cin, taps, head, b, c, step, mask, *sums)
    outs = [struct((tokens, 384), bf16), struct((8, 256)), struct((8, 128))]
    return call(
        tail_kernel,
        outs,
        in_specs=[SMEM] + [whole(a.shape) for a in args],
        out_specs=[whole(o.shape) for o in outs],
        scratch=[pltpu.VMEM((tokens + 8, 256), f32), pltpu.VMEM((8, 256), f32)],
        name="tail",
        flops=2 * tokens * 128 * 128 * 4,
        size=8e6,
    )(sm, *args)


def term_kernel(sm, nt_ref, *refs):
    *parts, out_ref = refs
    at = 0
    for part in parts:
        out_ref[:, at : at + part.shape[1]] = dot(nt_ref[...], part[...]).astype(bf16)
        at += part.shape[1]


def in_term(half, normt, parts, name):
    halves, width, tokens = normt.shape
    n = sum(p.shape[1] for p in parts)
    spec = pltpu.PrefetchScalarGridSpec(
        num_scalar_prefetch=1,
        grid=(1,),
        in_specs=[pl.BlockSpec((None, width, tokens), lambda g, sm: (sm[0], 0, 0))]
        + [pl.BlockSpec(p.shape, lambda g, sm: (0, 0)) for p in parts],
        out_specs=pl.BlockSpec((width, n), lambda g, sm: (0, 0)),
    )
    return pl.pallas_call(
        term_kernel,
        out_shape=struct((width, n), bf16),
        grid_spec=spec,
        name=name,
        compiler_params=pltpu.CompilerParams(vmem_limit_bytes=VMEM_LIMIT, dimension_semantics=("arbitrary",)),
        cost_estimate=pl.CostEstimate(
            flops=2 * tokens * width * n, bytes_accessed=2 * (width * tokens + tokens * n + width * n), transcendentals=0
        ),
    )(half, normt, *parts)


def last_kernel(count, x_ref, cot_ref, gain_ref, *refs):
    ds, ws, (dx_ref, gg_ref) = refs[:count], refs[count : 2 * count], refs[2 * count :]
    x = x_ref[...]
    width = x.shape[1]
    dn = functools.reduce(jnp.add, [dot_nt(d[...], w[...]) for d, w in zip(ds, ws)])
    r = lax.rsqrt(jnp.mean(x * x, axis=-1, keepdims=True) + EPS)
    u = dn * gain_ref[0:1, :]
    xr = x * r
    mu = jnp.sum(u * xr, axis=-1, keepdims=True) * (1.0 / width)
    dx_ref[...] = cot_ref[...] + r * (u - xr * mu)
    gg = rows8(dn * xr)

    @pl.when(pl.program_id(0) == 0)
    def _():
        gg_ref[...] = gg

    @pl.when(pl.program_id(0) > 0)
    def _():
        gg_ref[...] += gg


def last(x, cot, gain, pairs):
    tokens, width = x.shape
    row = lambda n: pl.BlockSpec((MID, n), lambda g: (g, 0))
    ds, ws = zip(*pairs)
    n = sum(k for _, k, _ in ds)
    return call(
        functools.partial(last_kernel, len(pairs)),
        [struct(x.shape), struct((8, width))],
        grid=(tokens // MID,),
        in_specs=[row(width), row(width), whole(gain.shape)]
        + [pl.BlockSpec((MID, k), functools.partial(lambda i, g: (g, i), i)) for _, k, i in ds]
        + [pl.BlockSpec((width, k), functools.partial(lambda i, g: (0, i), i)) for _, k, i in ws],
        out_specs=[row(width), whole((8, width))],
        name="last",
        flops=2 * tokens * width * n,
        size=40e6,
    )(x, cot, gain, *[d[0] for d in ds], *[w[0] for w in ws])


Y, CORE, X, Z1, Z2 = 1, 2, 4, 8, 16


def exchange(a, bit):
    return lax.ppermute(a, AXES, [(i, i ^ bit) for i in range(SHARDS)])


def gather_z(own):
    two = jnp.concatenate([own, exchange(own, Z1)], axis=0)
    return jnp.concatenate([two, exchange(two, Z2)], axis=0)


def gather_rest(four, x_first):
    first, second = (X, Y) if x_first else (Y, X)
    found = {0: four, first: exchange(four, first)}
    for key in (0, first):
        found[key | second] = exchange(found[key], second)
    for key in (0, X, Y, X | Y):
        found[key | CORE] = exchange(found[key], CORE)
    return [found[key] for key in PIECES]


def take(a, bit, axis):
    return lax.dynamic_index_in_dim(a, bit, axis, keepdims=False)


def scatter_chips(place, keep, order):
    names = [Z2, Z1, X, Y]
    left = keep.reshape(2, 2, 2, 2, keep.shape[0] // 16, keep.shape[1])
    for bit in order:
        axis = names.index(bit)
        names.pop(axis)
        mine = jnp.where((place & bit) > 0, 1, 0)
        got = exchange(take(left, 1 - mine, axis), bit)
        left = take(left, mine, axis).astype(f32) + got.astype(f32)
        if names:
            left = left.astype(bf16)
    return left


def both(a, b):
    return (a.astype(f32) + b.astype(f32)).astype(bf16)


def pad_to(a, rows, columns):
    return jnp.pad(a, ((0, rows - a.shape[0]), (0, columns - a.shape[1])))


def local(
    ring, block_input, cotangent, scene_lengths, norm_gain, in_weight, conv_weight, conv_bias, dt_bias, a_log, skip_gain,
    gated_gain, out_weight,
):
    tokens, width = block_input.shape
    heads = a_log.shape[0]
    inner = out_weight.shape[0] * lax.axis_size(AXES)
    channels = conv_bias.shape[0] * lax.axis_size(AXES)
    proj = in_weight.shape[1]
    bc = proj - 2 * inner
    place = lax.axis_index(AXES).astype(jnp.int32)
    bounds = jnp.cumsum(scene_lengths[0]).astype(jnp.int32)
    sm = jnp.concatenate([bounds, place[None], jnp.zeros((4,), jnp.int32)])
    groups = inner // GROUP
    gather = lambda a: lax.all_gather(a.astype(bf16), AXES, axis=0, tiled=True)
    skip_row = jnp.repeat(skip_gain, inner // heads)[None]
    w_low = in_weight.astype(bf16)
    if ring:
        out_full = gather(out_weight)
        small = jnp.concatenate(
            [
                jnp.concatenate([norm_gain, gated_gain])[None],
                pad_to(conv_weight.T, 4, 96),
                pad_to(conv_bias[None], 27, 96),
            ],
            axis=0,
        )
        first = jnp.concatenate([w_low[:, 2 * inner :], small.astype(bf16)], axis=1)
        pieces = gather_rest(gather_z(first), True)
        w_bc, taps, gain = unpack(sm, pieces, skip_row, channels, width)
        bases = (0, groups // 2)
        weights = []
        wide = inner // 2
        for base in bases:
            at = base * GROUP
            four = gather_z(jnp.concatenate([w_low[:, at : at + wide], w_low[:, inner + at : inner + at + wide]], axis=1))
            weights.append((gather_rest(four[:, :wide], True), gather_rest(four[:, wide:], False)))
    else:
        in_full, out_full = gather(in_weight), gather(out_weight)
        norm_full, conv_full, bias_full, gated_full = map(gather, (norm_gain, conv_weight, conv_bias, gated_gain))
        gain = jnp.broadcast_to(norm_full.astype(f32)[None], (8, width))
        w_bc = pad_to(in_full[:, 2 * inner :], width, 384)
        taps = jnp.concatenate(
            [
                conv_full.astype(f32).T,
                bias_full.astype(f32)[None],
                pad_to(jnp.concatenate([skip_row, gated_full.astype(f32)[None]], axis=0), 3, channels),
            ],
            axis=0,
        )
        bases = (0,)
        weights = [([in_full], [in_full])]
    taps_bc = taps[:, inner:]
    head = jnp.pad(jnp.stack([dt_bias, jnp.exp(a_log)]), ((0, 6), (0, 128 - heads)))
    (normed, normt, cin_bc, b, c, bt, ct, s, st, cum, cumt, ea, eb, step, mask) = prep(
        ring, sm, block_input, gain, w_bc, taps_bc, head, heads
    )
    cumt = cumt.reshape(heads // 4, 4, tokens)
    count = groups // len(bases)
    pre = (ea, eb, cum, cumt, c, bt, s, mask)
    runs = [fwd(base, count, ring, sm, normed, *w, inner, taps, pre) for base, w in zip(bases, weights)]
    mixed, dz, dy, gg, *terms = mid(
        ring, sm, cotangent, out_full, taps, mask, [r[0] for r in runs], [r[2] for r in runs]
    )
    normt = normt.reshape(2 if ring else 1, -1, tokens)
    core = sm[3:4] >> 1 & 1
    if ring:
        gate_away = exchange(in_term(1 - core, normt, [dz], "gate_away"), CORE)
        out_away = exchange(terms[1], CORE)
        gate_here = in_term(core, normt, [dz], "gate_here")
        early = jnp.concatenate([both(gate_here, gate_away), both(terms[0], out_away)], axis=1)
        early = lax.psum_scatter(early, CHIPS, scatter_dimension=0, tiled=True).astype(f32)
        gate_grad, out_grad = early[:, :inner], early[:, inner:]
        out_grad = jnp.concatenate([out_grad[:, :width], out_grad[:, width:]], axis=0)
    dvs, grads, sums = [], [], []
    pre = (ea, eb, cum, cumt, b, c, ct, st, mask)
    for base, run in zip(bases, runs):
        dv, grad, *part = bwd(base, count, run[1], run[2], dy, taps, pre, run[3])
        dvs.append(dv)
        grads.append(grad)
        sums += part
    dbc, grad_bc, stat = tail(sm, cin_bc, taps_bc, head, b, c, step, mask, sums)
    grads = jnp.concatenate([*grads, grad_bc], axis=1)
    if ring:
        late = []
        for parts, order, name in (([dvs[0]], (X, Y, Z2, Z1), "late0"), ([dvs[1], dbc], (Y, X, Z2, Z1), "late1")):
            away = exchange(in_term(1 - core, normt, parts, name + "_away"), CORE)
            here = in_term(core, normt, parts, name + "_here")
            late.append(scatter_chips(place, both(here, away), order))
        in_grad = jnp.concatenate([gate_grad, *late], axis=1)[:, :proj]
        pairs = []
        for i, run in enumerate(runs):
            pairs.append(((dz, wide, i), (run[4], wide, 0)))
            pairs.append(((dvs[i], wide, 0), (run[5], wide, 0)))
    else:
        scatter = lambda a: lax.psum_scatter(a.astype(f32), AXES, scatter_dimension=0, tiled=True)
        in_grad = scatter(in_term(core * 0, normt, [dz, *dvs, dbc], "all")[:, :proj])
        out_grad = scatter(terms[0])
        pairs = [((dz, inner, 0), (in_full, inner, 0)), ((dvs[0], inner, 0), (in_full, inner, 1))]
    pairs.append(((dbc, 384, 0), (w_bc, 384, 0)))
    input_grad, d_gain = last(block_input, cotangent, gain, pairs)
    block_output = branch(block_input, mixed, out_full)
    d_skip = jnp.sum(grads[5, :inner].reshape(heads, -1), axis=1)
    side = jnp.concatenate([jnp.sum(d_gain, axis=0), stat[0, :heads], stat[1, :heads], d_skip])
    small = jnp.concatenate(
        [grads[:5], pad_to(jnp.sum(gg, axis=0)[None], 1, channels), pad_to(side[None], 2, channels)], axis=0
    )
    if ring:
        for bit in (CORE, X, Y, Z1, Z2):
            small = small + exchange(small, bit)
    else:
        small = lax.psum(small, AXES)
    part = lambda row, n: lax.dynamic_slice_in_dim(row, place * n, n, axis=-1)
    side = small[6, width:]
    return (
        block_output,
        input_grad,
        part(small[6], norm_gain.shape[0]),
        in_grad,
        part(small[:4], conv_bias.shape[0]).T,
        part(small[4], conv_bias.shape[0]),
        side[:heads],
        side[heads : 2 * heads],
        side[2 * heads : 3 * heads],
        part(small[5], gated_gain.shape[0]),
        out_grad,
    )


def solution(mesh):
    dp, fsdp = mesh.devices.shape
    split = jax.sharding.Mesh(mesh.devices.reshape(dp // 2, 2, fsdp), AXES)
    row = P(AXES, None)
    flat = P(AXES)
    return jax.shard_map(
        functools.partial(local, (dp, fsdp) == (16, 2)),
        mesh=split,
        in_specs=(row, row, row, flat, row, row, flat, P(), P(), P(), flat, row),
        out_specs=(row, row, flat, row, row, flat, P(), P(), P(), flat, row),
        check_vma=False,
    )
```

time: 1020 us -> 452 us (0.44)
  matrix products: 308 us -> 0 us
  Pallas kernels: 0 us -> 237 us
  waiting for transfers between devices: 305 us -> 106 us
  blocking collectives: 150 us -> 0 us
  other arithmetic: 147 us -> 20.6 us
  local copies, waits for them, and re-layouts: 90.8 us -> 13 us
  starting transfers between devices: 0.16 us -> 53.9 us
    dot_general x18 -> x0, matrix products: 308 us -> none  [the longest x3 133 us: mixer(): jnp.einsum('bhts,bshp->bthp', scores, block_values, precision=highest)]
    reduce_scatter x2 -> x1, waiting for transfers between devices: 305 us -> 0.02 us  [local(): lax.psum_scatter(early, CHIPS, scatter_dimension=0, tiled=True).astype(f32)]
    pallas_call x0 -> x16, Pallas kernels: none -> 237 us  [the longest x2 67.1 us: bwd(): call(functools.partial(bwd_kernel, base), [struct((tokens, count * GROUP)...]
    ppermute x0 -> x58, waiting for transfers between devices: none -> 106 us  [exchange(): return lax.ppermute(a, AXES, [(i, i ^ bit) for i in range(SHARDS)])]
    unnamed x2 -> x0, blocking collectives: 83.1 us -> none
    all_gather x1 -> x0, blocking collectives: 66.8 us -> none  [local(): lax.all_gather(conv_weight.astype(jnp.bfloat16), ('dp', 'fsdp'), axis=0,...]
    reduce_sum x10 -> x3, other arithmetic: 67.2 us -> 0.91 us  [the longest x1 0.77 us: local(): jnp.sum(d_gain, axis=0)]
    ppermute x0 -> x58, starting transfers between devices: none -> 53.8 us  [exchange(): return lax.ppermute(a, AXES, [(i, i ^ bit) for i in range(SHARDS)])]
  transfers between devices with their start and end apart: 4 -> 60, of which waited for: 1 -> 20; matrix products, arithmetic and copies ran while one was open for 41% -> 5% of each run, Pallas kernels for 0% -> 46%
where the time goes in v1:
time: 452 us; the launch traced here: 446 us
  Pallas kernels  237 us (52%)
  waiting for transfers between devices  106 us (23%)
  starting transfers between devices  53.9 us (12%)
  other arithmetic  20.6 us (5%)
  between operations  15.3 us (3%)
  local copies, waits for them, and re-layouts  13 us (3%)
    ppermute x58, waiting for transfers between devices, exchange(): return lax.ppermute(a, AXES, [(i, i ^ bit) for i in range(SHARDS)])  106 us
    pallas_call x2, Pallas kernels, bwd(): call(functools.partial(bwd_kernel, base), [struct((tokens, count * GROUP)...  67.1 us
    ppermute x58, starting transfers between devices, exchange(): return lax.ppermute(a, AXES, [(i, i ^ bit) for i in range(SHARDS)])  53.8 us
    pallas_call x2, Pallas kernels, fwd(): call(functools.partial(fwd_kernel, base, ring), outs, grid=(count,), in_s...  53 us
    pallas_call x1, Pallas kernels, mid(): call(functools.partial(mid_kernel, ring, len(zs)), outs, grid=(tokens //...  33.8 us
    pallas_call x6, Pallas kernels, in_term(): pl.pallas_call(term_kernel, out_shape=struct((width, n), bf16), grid_spec...  30.9 us
    pallas_call x1, Pallas kernels, last(): call(functools.partial(last_kernel, len(pairs)), [struct(x.shape), struct...  18.6 us
    pallas_call x1, Pallas kernels, prep(): call(functools.partial(prep_kernel, ring), outs, in_specs=[SMEM] + [whole...  13.1 us
  transfers between devices with their start and end apart: 60, of which 20 were waited for; matrix products, arithmetic and copies ran while one was open for 5% of the time, Pallas kernels for 46%

profile of v1, /device:TPU:0, one launch (start us, length us, event | category | flops | bytes accessed | tf_op | source)
XLA Modules:
  0.0 446.4 jit_solution(11088152035992461735)
XLA Ops:
  7.2 1.6 convert_element_type.146
  11.6 1.1 convert_element_type.147
  12.9 3.0 collective-permute-start
  16.0 2.1 collective-permute-start.25
  18.2 2.6 collective-permute-start.1
  20.8 3.9 collective-permute-done.9
  25.2 1.5 collective-permute-start.2
  26.7 1.5 collective-permute-start.3
  28.3 3.1 collective-permute-start.26
  31.9 9.0 %collective-permute-done.10 = bf16[64,2048]{1,0:T(8,128)(2,1)S(1)} collective-permute-done((bf16[64,2048]{1,0:T(8,128)(2,1)S(1)}, bf16[64,2048]{1,0:T(8,128)(2,1)S(1)}, u32[]{:S(2)}, u32[]{:S(2)}) %collective-permute-start.10) | collective-permute-done | bytes 262176 | tf_op jit(solution)/shard_map/ppermute | solution.py:757
  41.0 1.4 collective-permute-start.11
  42.5 1.2 collective-permute-start.12
  44.7 0.9 collective-permute-done.7.refs_6_
  45.6 1.5 collective-permute-start.18
  47.1 7.2 %collective-permute-start.19 = (bf16[128,1024]{1,0:T(8,128)(2,1)S(1)}, bf16[128,1024]{1,0:T(8,128)(2,1)}, u32[]{:S(2)}, u32[]{:S(2)}) collective-permute-start(bf16[128,1024]{1,0:T(8,128)(2,1)S(1)} %get-tuple-element.127.refs_9_), channel_id=1, source_target_pairs={{0,1},{1,0},{2,3},{3,2},{4,5},{5,4},{6,7},{7,6},{8,9},{9,8},{10,11... | collective-permute-start | bytes 786440 | tf_op jit(solution)/shard_map/ppermute | solution.py:757
  54.8 1.0 collective-permute-done.18.refs_10_
  55.9 7.2 %collective-permute-done.19.refs_11_ = bf16[128,1024]{1,0:T(8,128)(2,1)} collective-permute-done((bf16[128,1024]{1,0:T(8,128)(2,1)S(1)}, bf16[128,1024]{1,0:T(8,128)(2,1)}, u32[]{:S(2)}, u32[]{:S(2)}) %collective-permute-start.19) | collective-permute-done | bytes 262176 | tf_op jit(solution)/shard_map/ppermute | solution.py:757
  63.6 3.2 collective-permute-start.35
  66.9 1.6 collective-permute-done.28.refs_3_
  68.5 2.2 collective-permute-start.13
  71.3 2.9 collective-permute-done.35.refs_11_
  74.6 9.1 %collective-permute-done.13.refs_4_ = bf16[128,1024]{1,0:T(8,128)(2,1)S(1)} collective-permute-done((bf16[128,1024]{1,0:T(8,128)(2,1)S(1)}, bf16[128,1024]{1,0:T(8,128)(2,1)S(1)}, u32[]{:S(2)}, u32[]{:S(2)}) %collective-permute-start.13) | collective-permute-done | bytes 262176 | tf_op jit(solution)/shard_map/ppermute | solution.py:757
  85.4 2.5 collective-permute-start.29
  90.8 3.0 unpack.1
  93.8 1.3 slice.93.taps_ref
  95.1 13.1 %prep.1 = (bf16[1024,1024]{1,0:T(8,128)(2,1)}, bf16[1024,1024]{1,0:T(8,128)(2,1)}, bf16[1024,256]{1,0:T(8,128)(2,1)}, bf16[1024,128]{1,0:T(8,128)(2,1)}, bf16[10...) custom-call(s32[8]{0:T(128)} %pad_add_fusion.sm.refs_0_, ...), custom_call_target="tpu_custom_call" | custom-call | flops 805306368 | bytes 12000000 | tf_op jit(solution)/shard_map/prep/pallas_call | solution.py:230
  108.3 1.6 reshape.85.refs_22_.cumt_ref
  111.0 26.5 %fwd0.1 = (bf16[1024,1024]{1,0:T(8,128)(2,1)}, bf16[1024,1024]{1,0:T(8,128)(2,1)}, f32[1024,1024]{1,0:T(8,128)}, bf16[1024,1024]{1,0:T(8,128)(2,1)}, bf16[1024,1...) custom-call(s32[8]{0:T(128)} %pad_add_fusion.sm.refs_0_, bf16[128,1024]{1,0:T(8,128)(2,1)} %copy-done.5, ...), custom_call_target="tpu_custom_call" | custom-call | flops 12884901888 | bytes 16000000 | tf_op jit(solution)/shard_map/fwd0/pallas_call | solution.py:346
  139.1 26.5 %fwd4.1 = (bf16[1024,1024]{1,0:T(8,128)(2,1)}, bf16[1024,1024]{1,0:T(8,128)(2,1)}, f32[1024,1024]{1,0:T(8,128)}, bf16[1024,1024]{1,0:T(8,128)(2,1)}, bf16[1024,1...) custom-call(s32[8]{0:T(128)} %pad_add_fusion.sm.refs_0_, bf16[128,1024]{1,0:T(8,128)(2,1)} %copy-done.7, ...), custom_call_target="tpu_custom_call" | custom-call | flops 12884901888 | bytes 16000000 | tf_op jit(solution)/shard_map/fwd4/pallas_call | solution.py:346
  165.7 33.8 %mid.1 = (bf16[1024,2048]{1,0:T(8,128)(2,1)}, bf16[1024,2048]{1,0:T(8,128)(2,1)}, bf16[1024,2048]{1,0:T(8,128)(2,1)}, f32[8,2048]{1,0:T(8,128)}, bf16[512,2048]{1,0:T(8,128)(2,1)}, /*index=5*/bf16[512,2048]{1,0:T(8,128)(2,1)}) custom-call(s32[8]{0:T(128)} %pad_add_fusion.sm.refs_0_, f32[1024,1024]{1,0:T(8,128)} %cot_ref.3, ...), custom_call_target="tpu_custom_call" | custom-call | flops 8589934592 | bytes 30000000 | tf_op jit(solution)/shard_map/mid/pallas_call | solution.py:456
  200.0 6.2 %gate_away.1 = bf16[512,2048]{1,0:T(8,128)(2,1)} custom-call(s32[1]{0:T(128)S(6)} %sub.10.sm, bf16[2,512,1024]{2,1,0:T(8,128)(2,1)} %bitcast.80, bf16[1024,2048]{1,0:T(8,128)(2,1)} %get-tuple-element.83.refs_0_.refs_2_), custom_call_target="tpu_custom_call" | custom-call | flops 2147483648 | bytes 7340032 | tf_op jit(solution)/shard_map/gate_away/pallas_call | solution.py:701
  206.3 33.6 %bwd0.1 = (bf16[1024,1024]{1,0:T(8,128)(2,1)}, f32[8,1024]{1,0:T(8,128)}, f32[1024,128]{1,0:T(8,128)}, f32[1024,128]{1,0:T(8,128)}, f32[1024,128]{1,0:T(8,128)},...) custom-call(bf16[1024,1024]{1,0:T(8,128)(2,1)} %get-tuple-element.84.cin_ref, f32[1024,1024]{1,0:T(8,128)} %get-tuple-element.80.refs_2_.y_ref, ...), custom_call_target="tpu_custom_call" | custom-call | flops 2147483648 | bytes 16000000 | tf_op jit(solution)/shard_map/bwd0/pallas_call | solution.py:591
  239.8 33.5 %bwd4.1 = (bf16[1024,1024]{1,0:T(8,128)(2,1)}, f32[8,1024]{1,0:T(8,128)}, f32[1024,128]{1,0:T(8,128)}, f32[1024,128]{1,0:T(8,128)}, f32[1024,128]{1,0:T(8,128)},...) custom-call(bf16[1024,1024]{1,0:T(8,128)(2,1)} %get-tuple-element.91.cin_ref, f32[1024,1024]{1,0:T(8,128)} %get-tuple-element.81.refs_3_.y_ref, ...), custom_call_target="tpu_custom_call" | custom-call | flops 2147483648 | bytes 16000000 | tf_op jit(solution)/shard_map/bwd4/pallas_call | solution.py:591
  273.4 0.8 fusion.7
  274.2 8.2 %tail.1 = (bf16[1024,384]{1,0:T(8,128)(2,1)}, f32[8,256]{1,0:T(8,128)}, f32[8,128]{1,0:T(8,128)}) custom-call(s32[8]{0:T(128)} %pad_add_fusion.sm.refs_0_, bf16[1024,256]{1,0:T(8,128)(2,1)} %get-tuple-element.94.cin_ref, f32[8,256]{1,0:T(8,128)} %slice.93.taps_ref, f32[8,128]{1,0:T(8,128)} %select_maximum_fusion.4.head_ref, ...), custom_call_target="tpu_custom_call" | custom-call | flops 134217728 | bytes 8000000 | tf_op jit(solution)/shard_map/tail/pallas_call | solution.py:671
  282.5 6.3 %gate_here.1 = bf16[512,2048]{1,0:T(8,128)(2,1)} custom-call(s32[1]{0:T(128)S(6)} %and.22.sm, bf16[2,512,1024]{2,1,0:T(8,128)(2,1)} %bitcast.81, bf16[1024,2048]{1,0:T(8,128)(2,1)} %get-tuple-element.83.refs_0_.refs_2_), custom_call_target="tpu_custom_call" | custom-call | flops 2147483648 | bytes 7340032 | tf_op jit(solution)/shard_map/gate_here/pallas_call | solution.py:701
  288.8 2.6 add_convert_fusion
  291.5 2.4 add_convert_fusion.1
  293.8 2.4 pad_maximum_fusion
  296.3 18.6 %last.1 = (f32[1024,1024]{1,0:T(8,128)}, f32[8,1024]{1,0:T(8,128)}) custom-call(f32[1024,1024]{1,0:T(8,128)} %x_ref.5, f32[1024,1024]{1,0:T(8,128)} %cot_ref.3, f32[8,1024]{1,0:T(8,128)} %get-tuple-element.67.gain_ref, bf16[1024,2048]{1,0:T(8,128)(2,1)} %get-tuple-element.83.refs_0_.refs_2_, bf16[1024,1024]{1,0:T(8,128)(2,1)} %get-tuple-element.90.refs_1_.refs_0_, ...), custom_call_target="tpu_custom_call" | custom-call | flops 9395240960 | bytes 40000000 | tf_op jit(solution)/shard_map/last/pallas_call | solution.py:739
  317.3 5.0 %late1_away.1 = bf16[512,1408]{1,0:T(8,128)(2,1)} custom-call(s32[1]{0:T(128)S(6)} %sub.10.sm, bf16[2,512,1024]{2,1,0:T(8,128)(2,1)} %bitcast.82, bf16[1024,1024]{1,0:T(8,128)(2,1)} %get-tuple-element.93.refs_3_.refs_0_, bf16[1024,384]{1,0:T(8,128)(2,1)} %get-tuple-element.106.refs_4_.refs_1_), custom_call_target="tpu_custom_call" | custom-call | flops 1476395008 | bytes 5373952 | tf_op jit(solution)/shard_map/late1_away/pallas_call | solution.py:701
  322.4 1.6 collective-permute-start.42
  324.0 4.2 late0_away.1
  328.6 4.1 collective-permute-start.43
  332.7 9.7 %branch.1 = f32[1024,1024]{1,0:T(8,128)} custom-call(f32[1024,1024]{1,0:T(8,128)} %x_ref.5, bf16[1024,2048]{1,0:T(8,128)(2,1)} %get-tuple-element.82.m_ref, bf16[2048,1024]{1,0:T(8,128)(2,1)} %all-gather.2.cloned.1.call-done.w_ref), custom_call_target="tpu_custom_call" | custom-call | flops 4294967296 | bytes 16000000 | tf_op jit(solution)/shard_map/branch/pallas_call | solution.py:476
  342.5 5.0 %late1_here.1 = bf16[512,1408]{1,0:T(8,128)(2,1)} custom-call(s32[1]{0:T(128)S(6)} %and.22.sm, bf16[2,512,1024]{2,1,0:T(8,128)(2,1)} %bitcast.84, bf16[1024,1024]{1,0:T(8,128)(2,1)} %get-tuple-element.93.refs_3_.refs_0_, bf16[1024,384]{1,0:T(8,128)(2,1)} %get-tuple-element.106.refs_4_.refs_1_), custom_call_target="tpu_custom_call" | custom-call | flops 1476395008 | bytes 5373952 | tf_op jit(solution)/shard_map/late1_here/pallas_call | solution.py:701
  347.5 2.2 collective-permute-start.45
  349.8 4.2 late0_here.1
  353.9 1.7 collective-permute-done.45
  355.7 1.6 add_convert_fusion.3
  357.6 1.1 copy-done.1
  359.3 1.7 collective-permute-start.54
  362.8 13.0 %collective-permute-done.49 = bf16[2,2,2,32,1024]{4,3,1,0,2:T(8,128)(2,1)S(1)} collective-permute-done((bf16[2,2,2,32,1024]{4,3,1,0,2:T(8,128)(2,1)S(1)}, bf16[2,2,2,32,1024]{4,3,1,0,2:T(8,128)(2,1)S(1)}, u32[]{:S(2)}, u32[]{:S(2)}) %collective-permute-start.49) | collective-permute-done | bytes 524320 | tf_op jit(solution)/shard_map/ppermute | solution.py:757
  376.1 3.2 collective-permute-start.50
  379.3 30.0 %collective-permute-done.54 = bf16[2,2,2,32,1408]{4,3,1,0,2:T(8,128)(2,1)S(1)} collective-permute-done((bf16[2,2,2,32,1408]{4,3,1,0,2:T(8,128)(2,1)S(1)}, bf16[2,2,2,32,1408]{4,3,1,0,2:T(8,128)(2,1)S(1)}, u32[]{:S(2)}, u32[]{:S(2)}) %collective-permute-start.54) | collective-permute-done | bytes 720928 | tf_op jit(solution)/shard_map/ppermute | solution.py:757
  410.2 5.0 %collective-permute-done.50 = bf16[2,2,32,1024]{3,2,1,0:T(8,128)(2,1)S(1)} collective-permute-done((bf16[2,2,32,1024]{3,2,1,0:T(8,128)(2,1)S(1)}, bf16[2,2,32,1024]{3,2,1,0:T(8,128)(2,1)S(1)}, u32[]{:S(2)}, u32[]{:S(2)}) %collective-permute-start.50) | collective-permute-done | bytes 262176 | tf_op jit(solution)/shard_map/ppermute | solution.py:757
  415.5 4.3 collective-permute-done.55
  420.0 7.1 %collective-permute-done.51 = bf16[2,32,1024]{2,1,0:T(8,128)(2,1)S(1)} collective-permute-done((bf16[2,32,1024]{2,1,0:T(8,128)(2,1)S(1)}, bf16[2,32,1024]{2,1,0:T(8,128)(2,1)S(1)}, u32[]{:S(2)}, u32[]{:S(2)}) %collective-permute-start.51) | collective-permute-done | bytes 131104 | tf_op jit(solution)/shard_map/ppermute | solution.py:757
  427.2 3.7 collective-permute-done.56
  431.1 1.1 collective-permute-done.52
  432.3 3.3 collective-permute-done.57
  435.7 0.9 fusion.15
  437.3 0.9 slice.130
  438.2 0.8 pad_maximum_fusion.1
  (232 shorter events, 23.6 us)
Async XLA Ops:
  7.2 158.5 %all-gather.2.cloned.1.call-start = ((), (), s32[]{:S(2)}) async-start(), calls=%async_computation.1 | async-start | bytes 4325376 | tf_op jit(solution)/shard_map/all_gather | solution.py:815
  8.9 426.8 %reduce-scatter.2.cloned.1.call-start = ((), (), s32[]{:S(2)}) async-start(), calls=%async_computation.2 | async-start | bytes 4456448 | tf_op jit(solution)/shard_map/reduce_scatter | solution.py:872
  12.9 5.2 %collective-permute-start = (bf16[32,384]{1,0:T(8,128)(2,1)S(1)}, bf16[32,384]{1,0:T(8,128)(2,1)S(1)}, u32[]{:S(2)}, u32[]{:S(2)}) collective-permute-start(bf16[32,384]{1,0:T(8,128)(2,1)S(1)} %maximum_maximum_fusion), channel_id=1, source_target_pairs={{0,8},{1,9},{2,10},{3,11},{4,12},{5,13},{6,14},{7,15},{8,0},{9,1},... | collective-permute-start | bytes 73736 | tf_op jit(solution)/shard_map/ppermute | solution.py:757
  15.9 8.8 %collective-permute-start.9 = (bf16[32,2048]{1,0:T(8,128)(2,1)S(1)}, bf16[32,2048]{1,0:T(8,128)(2,1)S(1)}, u32[]{:S(2)}, u32[]{:S(2)}) collective-permute-start(bf16[32,2048]{1,0:T(8,128)(2,1)S(1)} %pad_maximum_fusion.8), channel_id=1, source_target_pairs={{0,8},{1,9},{2,10},{3,11},{4,12},{5,13},{6,14},{7,15},{8,0},{9,1},... | collective-permute-start | bytes 393224 | tf_op jit(solution)/shard_map/ppermute | solution.py:757
  16.0 12.2 %collective-permute-start.25 = (bf16[32,2048]{1,0:T(8,128)(2,1)S(1)}, bf16[32,2048]{1,0:T(8,128)(2,1)S(1)}, u32[]{:S(2)}, u32[]{:S(2)}) collective-permute-start(bf16[32,2048]{1,0:T(8,128)(2,1)S(1)} %pad_maximum_fusion.9), channel_id=1, source_target_pairs={{0,8},{1,9},{2,10},{3,11},{4,12},{5,13},{6,14},{7,15},{8,0},{9,1},... | collective-permute-start | bytes 393224 | tf_op jit(solution)/shard_map/ppermute | solution.py:757
  18.2 6.9 %collective-permute-start.1 = (bf16[64,384]{1,0:T(8,128)(2,1)S(1)}, bf16[64,384]{1,0:T(8,128)(2,1)S(1)}, u32[]{:S(2)}, u32[]{:S(2)}) collective-permute-start(bf16[64,384]{1,0:T(8,128)(2,1)S(1)} %pad_maximum_fusion.11), channel_id=1, source_target_pairs={{0,16},{1,17},{2,18},{3,19},{4,20},{5,21},{6,22},{7,23},{8,24},{9,... | collective-permute-start | bytes 147464 | tf_op jit(solution)/shard_map/ppermute | solution.py:757
  24.7 16.2 %collective-permute-start.10 = (bf16[64,2048]{1,0:T(8,128)(2,1)S(1)}, bf16[64,2048]{1,0:T(8,128)(2,1)S(1)}, u32[]{:S(2)}, u32[]{:S(2)}) collective-permute-start(bf16[64,2048]{1,0:T(8,128)(2,1)S(1)} %pad_maximum_fusion.5), channel_id=1, source_target_pairs={{0,16},{1,17},{2,18},{3,19},{4,20},{5,21},{6,22},{7,23},{8,24},{9,... | collective-permute-start | bytes 786440 | tf_op jit(solution)/shard_map/ppermute | solution.py:757
  25.2 6.3 %collective-permute-start.2 = (bf16[128,384]{1,0:T(8,128)(2,1)S(1)}, bf16[128,384]{1,0:T(8,128)(2,1)S(1)}, u32[]{:S(2)}, u32[]{:S(2)}) collective-permute-start(bf16[128,384]{1,0:T(8,128)(2,1)S(1)} %pad_maximum_fusion.10.refs_0_), channel_id=1, source_target_pairs={{0,4},{1,5},{2,6},{3,7},{4,0},{5,1},{6,2},{7,3},{8,12},{9,13},{10,... | collective-permute-start | bytes 294920 | tf_op jit(solution)/shard_map/ppermute | solution.py:757
  26.7 14.3 %collective-permute-start.3 = (bf16[128,384]{1,0:T(8,128)(2,1)S(1)}, bf16[128,384]{1,0:T(8,128)(2,1)S(1)}, u32[]{:S(2)}, u32[]{:S(2)}) collective-permute-start(bf16[128,384]{1,0:T(8,128)(2,1)S(1)} %pad_maximum_fusion.10.refs_0_), channel_id=1, source_target_pairs={{0,1},{1,0},{2,3},{3,2},{4,5},{5,4},{6,7},{7,6},{8,9},{9,8},{10,11... | collective-permute-start | bytes 294920 | tf_op jit(solution)/shard_map/ppermute | solution.py:757
  28.2 14.3 %collective-permute-start.5 = (bf16[128,384]{1,0:T(8,128)(2,1)S(1)}, bf16[128,384]{1,0:T(8,128)(2,1)S(1)}, u32[]{:S(2)}, u32[]{:S(2)}) collective-permute-start(bf16[128,384]{1,0:T(8,128)(2,1)S(1)} %pad_maximum_fusion.10.refs_0_), channel_id=1, source_target_pairs={{0,2},{1,3},{2,0},{3,1},{4,6},{5,7},{6,4},{7,5},{8,10},{9,11},{10,... | collective-permute-start | bytes 294920 | tf_op jit(solution)/shard_map/ppermute | solution.py:757
  28.3 15.6 %collective-permute-start.26 = (bf16[64,2048]{1,0:T(8,128)(2,1)S(1)}, bf16[64,2048]{1,0:T(8,128)(2,1)S(1)}, u32[]{:S(2)}, u32[]{:S(2)}) collective-permute-start(bf16[64,2048]{1,0:T(8,128)(2,1)S(1)} %pad_maximum_fusion.6), channel_id=1, source_target_pairs={{0,16},{1,17},{2,18},{3,19},{4,20},{5,21},{6,22},{7,23},{8,24},{9,... | collective-permute-start | bytes 786440 | tf_op jit(solution)/shard_map/ppermute | solution.py:757
  31.5 12.5 %collective-permute-start.4 = (bf16[128,384]{1,0:T(8,128)(2,1)S(1)}, bf16[128,384]{1,0:T(8,128)(2,1)S(1)}, u32[]{:S(2)}, u32[]{:S(2)}) collective-permute-start(bf16[128,384]{1,0:T(8,128)(2,1)S(1)} %collective-permute-done.2.refs_1_), channel_id=1, source_target_pairs={{0,1},{1,0},{2,3},{3,2},{4,5},{5,4},{6,7},{7,6},{8,9},{9,8},{10,11... | collective-permute-start | bytes 294920 | tf_op jit(solution)/shard_map/ppermute | solution.py:757
  40.9 3.6 collective-permute-start.6
  41.0 67.2 %copy-start.4 = (bf16[128,1024]{1,0:T(8,128)(2,1)}, bf16[128,1024]{1,0:T(8,128)(2,1)S(1)}, u32[]{:S(2)}) copy-start(bf16[128,1024]{1,0:T(8,128)(2,1)S(1)} %get-tuple-element.127.refs_9_) | copy-start | bytes 786436
  41.0 67.2 %copy-start.5 = (bf16[128,1024]{1,0:T(8,128)(2,1)}, bf16[128,1024]{1,0:T(8,128)(2,1)S(1)}, u32[]{:S(2)}) copy-start(bf16[128,1024]{1,0:T(8,128)(2,1)S(1)} %get-tuple-element.128.refs_1_) | copy-start | bytes 786436
  41.0 13.2 %collective-permute-start.11 = (bf16[128,1024]{1,0:T(8,128)(2,1)S(1)}, bf16[128,1024]{1,0:T(8,128)(2,1)S(1)}, u32[]{:S(2)}, u32[]{:S(2)}) collective-permute-start(bf16[128,1024]{1,0:T(8,128)(2,1)S(1)} %get-tuple-element.128.refs_1_), channel_id=1, source_target_pairs={{0,4},{1,5},{2,6},{3,7},{4,0},{5,1},{6,2},{7,3},{8,12},{9,13},{10,... | collective-permute-start | bytes 786440 | tf_op jit(solution)/shard_map/ppermute | solution.py:757
  42.5 11.8 %collective-permute-start.12 = (bf16[128,1024]{1,0:T(8,128)(2,1)S(1)}, bf16[128,1024]{1,0:T(8,128)(2,1)S(1)}, u32[]{:S(2)}, u32[]{:S(2)}) collective-permute-start(bf16[128,1024]{1,0:T(8,128)(2,1)S(1)} %get-tuple-element.128.refs_1_), channel_id=1, source_target_pairs={{0,1},{1,0},{2,3},{3,2},{4,5},{5,4},{6,7},{7,6},{8,9},{9,8},{10,11... | collective-permute-start | bytes 786440 | tf_op jit(solution)/shard_map/ppermute | solution.py:757
  43.9 10.8 %collective-permute-start.14 = (bf16[128,1024]{1,0:T(8,128)(2,1)S(1)}, bf16[128,1024]{1,0:T(8,128)(2,1)S(1)}, u32[]{:S(2)}, u32[]{:S(2)}) collective-permute-start(bf16[128,1024]{1,0:T(8,128)(2,1)S(1)} %get-tuple-element.128.refs_1_), channel_id=1, source_target_pairs={{0,2},{1,3},{2,0},{3,1},{4,6},{5,7},{6,4},{7,5},{8,10},{9,11},{10,... | collective-permute-start | bytes 786440 | tf_op jit(solution)/shard_map/ppermute | solution.py:757
  44.0 1.6 collective-permute-start.7
  44.5 2.6 collective-permute-start.8
  44.7 63.5 %copy-start.6 = (bf16[128,1024]{1,0:T(8,128)(2,1)}, bf16[128,1024]{1,0:T(8,128)(2,1)S(1)}, u32[]{:S(2)}) copy-start(bf16[128,1024]{1,0:T(8,128)(2,1)S(1)} %get-tuple-element.125.refs_9_) | copy-start | bytes 786436
  44.7 63.5 %copy-start.7 = (bf16[128,1024]{1,0:T(8,128)(2,1)}, bf16[128,1024]{1,0:T(8,128)(2,1)S(1)}, u32[]{:S(2)}) copy-start(bf16[128,1024]{1,0:T(8,128)(2,1)S(1)} %get-tuple-element.126.refs_1_) | copy-start | bytes 786436
  45.6 10.3 %collective-permute-start.18 = (bf16[128,1024]{1,0:T(8,128)(2,1)S(1)}, bf16[128,1024]{1,0:T(8,128)(2,1)}, u32[]{:S(2)}, u32[]{:S(2)}) collective-permute-start(bf16[128,1024]{1,0:T(8,128)(2,1)S(1)} %get-tuple-element.127.refs_9_), channel_id=1, source_target_pairs={{0,4},{1,5},{2,6},{3,7},{4,0},{5,1},{6,2},{7,3},{8,12},{9,13},{10,... | collective-permute-start | bytes 786440 | tf_op jit(solution)/shard_map/ppermute | solution.py:757
  47.1 15.9 %collective-permute-start.19 = (bf16[128,1024]{1,0:T(8,128)(2,1)S(1)}, bf16[128,1024]{1,0:T(8,128)(2,1)}, u32[]{:S(2)}, u32[]{:S(2)}) collective-permute-start(bf16[128,1024]{1,0:T(8,128)(2,1)S(1)} %get-tuple-element.127.refs_9_), channel_id=1, source_target_pairs={{0,1},{1,0},{2,3},{3,2},{4,5},{5,4},{6,7},{7,6},{8,9},{9,8},{10,11... | collective-permute-start | bytes 786440 | tf_op jit(solution)/shard_map/ppermute | solution.py:757
  54.3 9.3 %collective-permute-start.21 = (bf16[128,1024]{1,0:T(8,128)(2,1)S(1)}, bf16[128,1024]{1,0:T(8,128)(2,1)}, u32[]{:S(2)}, u32[]{:S(2)}) collective-permute-start(bf16[128,1024]{1,0:T(8,128)(2,1)S(1)} %get-tuple-element.127.refs_9_), channel_id=1, source_target_pairs={{0,2},{1,3},{2,0},{3,1},{4,6},{5,7},{6,4},{7,5},{8,10},{9,11},{10,... | collective-permute-start | bytes 786440 | tf_op jit(solution)/shard_map/ppermute | solution.py:757
  54.3 12.6 %collective-permute-start.27 = (bf16[128,1024]{1,0:T(8,128)(2,1)S(1)}, bf16[128,1024]{1,0:T(8,128)(2,1)S(1)}, u32[]{:S(2)}, u32[]{:S(2)}) collective-permute-start(bf16[128,1024]{1,0:T(8,128)(2,1)S(1)} %get-tuple-element.126.refs_1_), channel_id=1, source_target_pairs={{0,4},{1,5},{2,6},{3,7},{4,0},{5,1},{6,2},{7,3},{8,12},{9,13},{10,... | collective-permute-start | bytes 786440 | tf_op jit(solution)/shard_map/ppermute | solution.py:757
  54.7 13.9 %collective-permute-start.28 = (bf16[128,1024]{1,0:T(8,128)(2,1)S(1)}, bf16[128,1024]{1,0:T(8,128)(2,1)S(1)}, u32[]{:S(2)}, u32[]{:S(2)}) collective-permute-start(bf16[128,1024]{1,0:T(8,128)(2,1)S(1)} %get-tuple-element.126.refs_1_), channel_id=1, source_target_pairs={{0,1},{1,0},{2,3},{3,2},{4,5},{5,4},{6,7},{7,6},{8,9},{9,8},{10,11... | collective-permute-start | bytes 786440 | tf_op jit(solution)/shard_map/ppermute | solution.py:757
  55.9 14.9 %collective-permute-start.30 = (bf16[128,1024]{1,0:T(8,128)(2,1)S(1)}, bf16[128,1024]{1,0:T(8,128)(2,1)S(1)}, u32[]{:S(2)}, u32[]{:S(2)}) collective-permute-start(bf16[128,1024]{1,0:T(8,128)(2,1)S(1)} %get-tuple-element.126.refs_1_), channel_id=1, source_target_pairs={{0,2},{1,3},{2,0},{3,1},{4,6},{5,7},{6,4},{7,5},{8,10},{9,11},{10,... | collective-permute-start | bytes 786440 | tf_op jit(solution)/shard_map/ppermute | solution.py:757
  63.0 7.9 %collective-permute-start.34 = (bf16[128,1024]{1,0:T(8,128)(2,1)S(1)}, bf16[128,1024]{1,0:T(8,128)(2,1)S(1)}, u32[]{:S(2)}, u32[]{:S(2)}) collective-permute-start(bf16[128,1024]{1,0:T(8,128)(2,1)S(1)} %get-tuple-element.125.refs_9_), channel_id=1, source_target_pairs={{0,4},{1,5},{2,6},{3,7},{4,0},{5,1},{6,2},{7,3},{8,12},{9,13},{10,... | collective-permute-start | bytes 786440 | tf_op jit(solution)/shard_map/ppermute | solution.py:757
  63.6 10.5 %collective-permute-start.35 = (bf16[128,1024]{1,0:T(8,128)(2,1)S(1)}, bf16[128,1024]{1,0:T(8,128)(2,1)S(1)}, u32[]{:S(2)}, u32[]{:S(2)}) collective-permute-start(bf16[128,1024]{1,0:T(8,128)(2,1)S(1)} %get-tuple-element.125.refs_9_), channel_id=1, source_target_pairs={{0,1},{1,0},{2,3},{3,2},{4,5},{5,4},{6,7},{7,6},{8,9},{9,8},{10,11... | collective-permute-start | bytes 786440 | tf_op jit(solution)/shard_map/ppermute | solution.py:757
  66.9 7.7 %collective-permute-start.37 = (bf16[128,1024]{1,0:T(8,128)(2,1)S(1)}, bf16[128,1024]{1,0:T(8,128)(2,1)S(1)}, u32[]{:S(2)}, u32[]{:S(2)}) collective-permute-start(bf16[128,1024]{1,0:T(8,128)(2,1)S(1)} %get-tuple-element.125.refs_9_), channel_id=1, source_target_pairs={{0,2},{1,3},{2,0},{3,1},{4,6},{5,7},{6,4},{7,5},{8,10},{9,11},{10,... | collective-permute-start | bytes 786440 | tf_op jit(solution)/shard_map/ppermute | solution.py:757
  68.5 15.2 %collective-permute-start.13 = (bf16[128,1024]{1,0:T(8,128)(2,1)S(1)}, bf16[128,1024]{1,0:T(8,128)(2,1)S(1)}, u32[]{:S(2)}, u32[]{:S(2)}) collective-permute-start(bf16[128,1024]{1,0:T(8,128)(2,1)S(1)} %collective-permute-done.11.refs_2_), channel_id=1, source_target_pairs={{0,1},{1,0},{2,3},{3,2},{4,5},{5,4},{6,7},{7,6},{8,9},{9,8},{10,11... | collective-permute-start | bytes 786440 | tf_op jit(solution)/shard_map/ppermute | solution.py:757
  70.7 14.6 %collective-permute-start.15 = (bf16[128,1024]{1,0:T(8,128)(2,1)S(1)}, bf16[128,1024]{1,0:T(8,128)(2,1)}, u32[]{:S(2)}, u32[]{:S(2)}) collective-permute-start(bf16[128,1024]{1,0:T(8,128)(2,1)S(1)} %collective-permute-done.11.refs_2_), channel_id=1, source_target_pairs={{0,2},{1,3},{2,0},{3,1},{4,6},{5,7},{6,4},{7,5},{8,10},{9,11},{10,... | collective-permute-start | bytes 786440 | tf_op jit(solution)/shard_map/ppermute | solution.py:757
  70.9 17.0 %collective-permute-start.16 = (bf16[128,1024]{1,0:T(8,128)(2,1)S(1)}, bf16[128,1024]{1,0:T(8,128)(2,1)}, u32[]{:S(2)}, u32[]{:S(2)}) collective-permute-start(bf16[128,1024]{1,0:T(8,128)(2,1)S(1)} %collective-permute-done.12.refs_3_), channel_id=1, source_target_pairs={{0,2},{1,3},{2,0},{3,1},{4,6},{5,7},{6,4},{7,5},{8,10},{9,11},{10,... | collective-permute-start | bytes 786440 | tf_op jit(solution)/shard_map/ppermute | solution.py:757
  74.1 14.5 %collective-permute-start.20 = (bf16[128,1024]{1,0:T(8,128)(2,1)}, bf16[128,1024]{1,0:T(8,128)(2,1)}, u32[]{:S(2)}, u32[]{:S(2)}) collective-permute-start(bf16[128,1024]{1,0:T(8,128)(2,1)} %collective-permute-done.19.refs_11_), channel_id=1, source_target_pairs={{0,4},{1,5},{2,6},{3,7},{4,0},{5,1},{6,2},{7,3},{8,12},{9,13},{10,... | collective-permute-start | bytes 786440 | tf_op jit(solution)/shard_map/ppermute | solution.py:757
  74.6 14.5 %collective-permute-start.22 = (bf16[128,1024]{1,0:T(8,128)(2,1)}, bf16[128,1024]{1,0:T(8,128)(2,1)}, u32[]{:S(2)}, u32[]{:S(2)}) collective-permute-start(bf16[128,1024]{1,0:T(8,128)(2,1)} %collective-permute-done.18.refs_10_), channel_id=1, source_target_pairs={{0,2},{1,3},{2,0},{3,1},{4,6},{5,7},{6,4},{7,5},{8,10},{9,11},{10,... | collective-permute-start | bytes 786440 | tf_op jit(solution)/shard_map/ppermute | solution.py:757
  83.7 5.4 %collective-permute-start.23 = (bf16[128,1024]{1,0:T(8,128)(2,1)}, bf16[128,1024]{1,0:T(8,128)(2,1)}, u32[]{:S(2)}, u32[]{:S(2)}) collective-permute-start(bf16[128,1024]{1,0:T(8,128)(2,1)} %collective-permute-done.19.refs_11_), channel_id=1, source_target_pairs={{0,2},{1,3},{2,0},{3,1},{4,6},{5,7},{6,4},{7,5},{8,10},{9,11},{10,... | collective-permute-start | bytes 786440 | tf_op jit(solution)/shard_map/ppermute | solution.py:757
  85.4 24.5 %collective-permute-start.29 = (bf16[128,1024]{1,0:T(8,128)(2,1)S(1)}, bf16[128,1024]{1,0:T(8,128)(2,1)}, u32[]{:S(2)}, u32[]{:S(2)}) collective-permute-start(bf16[128,1024]{1,0:T(8,128)(2,1)S(1)} %collective-permute-done.27.refs_2_), channel_id=1, source_target_pairs={{0,1},{1,0},{2,3},{3,2},{4,5},{5,4},{6,7},{7,6},{8,9},{9,8},{10,11... | collective-permute-start | bytes 786440 | tf_op jit(solution)/shard_map/ppermute | solution.py:757
  87.9 22.0 %collective-permute-start.31 = (bf16[128,1024]{1,0:T(8,128)(2,1)S(1)}, bf16[128,1024]{1,0:T(8,128)(2,1)}, u32[]{:S(2)}, u32[]{:S(2)}) collective-permute-start(bf16[128,1024]{1,0:T(8,128)(2,1)S(1)} %collective-permute-done.27.refs_2_), channel_id=1, source_target_pairs={{0,2},{1,3},{2,0},{3,1},{4,6},{5,7},{6,4},{7,5},{8,10},{9,11},{10,... | collective-permute-start | bytes 786440 | tf_op jit(solution)/shard_map/ppermute | solution.py:757
  88.6 21.8 %collective-permute-start.36 = (bf16[128,1024]{1,0:T(8,128)(2,1)}, bf16[128,1024]{1,0:T(8,128)(2,1)}, u32[]{:S(2)}, u32[]{:S(2)}) collective-permute-start(bf16[128,1024]{1,0:T(8,128)(2,1)} %copy-done.29), channel_id=1, source_target_pairs={{0,4},{1,5},{2,6},{3,7},{4,0},{5,1},{6,2},{7,3},{8,12},{9,13},{10,... | collective-permute-start | bytes 786440 | tf_op jit(solution)/shard_map/ppermute | solution.py:757
  89.1 21.4 %collective-permute-start.17 = (bf16[128,1024]{1,0:T(8,128)(2,1)}, bf16[128,1024]{1,0:T(8,128)(2,1)}, u32[]{:S(2)}, u32[]{:S(2)}) collective-permute-start(bf16[128,1024]{1,0:T(8,128)(2,1)} %copy-done.32), channel_id=1, source_target_pairs={{0,2},{1,3},{2,0},{3,1},{4,6},{5,7},{6,4},{7,5},{8,10},{9,11},{10,... | collective-permute-start | bytes 786440 | tf_op jit(solution)/shard_map/ppermute | solution.py:757
  89.1 21.8 %collective-permute-start.24 = (bf16[128,1024]{1,0:T(8,128)(2,1)}, bf16[128,1024]{1,0:T(8,128)(2,1)}, u32[]{:S(2)}, u32[]{:S(2)}) collective-permute-start(bf16[128,1024]{1,0:T(8,128)(2,1)} %collective-permute-done.20.refs_12_), channel_id=1, source_target_pairs={{0,2},{1,3},{2,0},{3,1},{4,6},{5,7},{6,4},{7,5},{8,10},{9,11},{10,... | collective-permute-start | bytes 786440 | tf_op jit(solution)/shard_map/ppermute | solution.py:757
  109.9 27.6 %collective-permute-start.39 = (bf16[128,1024]{1,0:T(8,128)(2,1)S(1)}, bf16[128,1024]{1,0:T(8,128)(2,1)S(1)}, u32[]{:S(2)}, u32[]{:S(2)}) collective-permute-start(bf16[128,1024]{1,0:T(8,128)(2,1)S(1)} %copy-done.30), channel_id=1, source_target_pairs={{0,2},{1,3},{2,0},{3,1},{4,6},{5,7},{6,4},{7,5},{8,10},{9,11},{10,... | collective-permute-start | bytes 786440 | tf_op jit(solution)/shard_map/ppermute | solution.py:757
  109.9 27.6 %collective-permute-start.32 = (bf16[128,1024]{1,0:T(8,128)(2,1)S(1)}, bf16[128,1024]{1,0:T(8,128)(2,1)S(1)}, u32[]{:S(2)}, u32[]{:S(2)}) collective-permute-start(bf16[128,1024]{1,0:T(8,128)(2,1)S(1)} %collective-permute-done.28.refs_3_), channel_id=1, source_target_pairs={{0,2},{1,3},{2,0},{3,1},{4,6},{5,7},{6,4},{7,5},{8,10},{9,11},{10,... | collective-permute-start | bytes 786440 | tf_op jit(solution)/shard_map/ppermute | solution.py:757
  110.4 27.1 %collective-permute-start.38 = (bf16[128,1024]{1,0:T(8,128)(2,1)S(1)}, bf16[128,1024]{1,0:T(8,128)(2,1)S(1)}, u32[]{:S(2)}, u32[]{:S(2)}) collective-permute-start(bf16[128,1024]{1,0:T(8,128)(2,1)S(1)} %copy-done.28), channel_id=1, source_target_pairs={{0,2},{1,3},{2,0},{3,1},{4,6},{5,7},{6,4},{7,5},{8,10},{9,11},{10,... | collective-permute-start | bytes 786440 | tf_op jit(solution)/shard_map/ppermute | solution.py:757
  110.5 27.1 %collective-permute-start.33 = (bf16[128,1024]{1,0:T(8,128)(2,1)}, bf16[128,1024]{1,0:T(8,128)(2,1)S(1)}, u32[]{:S(2)}, u32[]{:S(2)}) collective-permute-start(bf16[128,1024]{1,0:T(8,128)(2,1)} %collective-permute-done.29.refs_4_), channel_id=1, source_target_pairs={{0,2},{1,3},{2,0},{3,1},{4,6},{5,7},{6,4},{7,5},{8,10},{9,11},{10,... | collective-permute-start | bytes 786440 | tf_op jit(solution)/shard_map/ppermute | solution.py:757
  110.9 26.6 %collective-permute-start.40 = (bf16[128,1024]{1,0:T(8,128)(2,1)}, bf16[128,1024]{1,0:T(8,128)(2,1)S(1)}, u32[]{:S(2)}, u32[]{:S(2)}) collective-permute-start(bf16[128,1024]{1,0:T(8,128)(2,1)} %collective-permute-done.36.refs_12_), channel_id=1, source_target_pairs={{0,2},{1,3},{2,0},{3,1},{4,6},{5,7},{6,4},{7,5},{8,10},{9,11},{10,... | collective-permute-start | bytes 786440 | tf_op jit(solution)/shard_map/ppermute | solution.py:757
  199.5 89.3 %collective-permute-start.47 = (bf16[512,2048]{1,0:T(8,128)(2,1)}, bf16[512,2048]{1,0:T(8,128)(2,1)}, u32[]{:S(2)}, u32[]{:S(2)}) collective-permute-start(bf16[512,2048]{1,0:T(8,128)(2,1)} %get-tuple-element.120), channel_id=1, source_target_pairs={{0,2},{1,3},{2,0},{3,1},{4,6},{5,7},{6,4},{7,5},{8,10},{9,11},{10,... | collective-permute-start | bytes 6291464 | tf_op jit(solution)/shard_map/ppermute | solution.py:757
  206.2 85.3 %collective-permute-start.46 = (bf16[512,2048]{1,0:T(8,128)(2,1)}, bf16[512,2048]{1,0:T(8,128)(2,1)}, u32[]{:S(2)}, u32[]{:S(2)}) collective-permute-start(bf16[512,2048]{1,0:T(8,128)(2,1)} %gate_away.1), channel_id=1, source_target_pairs={{0,2},{1,3},{2,0},{3,1},{4,6},{5,7},{6,4},{7,5},{8,10},{9,11},{10,... | collective-permute-start | bytes 6291464 | tf_op jit(solution)/shard_map/ppermute | solution.py:757
  316.8 5.6 %collective-permute-start.41 = (f32[8,2304]{1,0:T(8,128)S(1)}, f32[8,2304]{1,0:T(8,128)S(1)}, u32[]{:S(2)}, u32[]{:S(2)}) collective-permute-start(f32[8,2304]{1,0:T(8,128)S(1)} %select_maximum_fusion), channel_id=1, source_target_pairs={{0,2},{1,3},{2,0},{3,1},{4,6},{5,7},{6,4},{7,5},{8,10},{9,11},{10,... | collective-permute-start | bytes 221192 | tf_op jit(solution)/shard_map/ppermute | solution.py:757
  322.3 35.3 %collective-permute-start.53 = (bf16[512,1408]{1,0:T(8,128)(2,1)}, bf16[512,1408]{1,0:T(8,128)(2,1)S(1)}, u32[]{:S(2)}, u32[]{:S(2)}) collective-permute-start(bf16[512,1408]{1,0:T(8,128)(2,1)} %late1_away.1), channel_id=1, source_target_pairs={{0,2},{1,3},{2,0},{3,1},{4,6},{5,7},{6,4},{7,5},{8,10},{9,11},{10,... | collective-permute-start | bytes 4325384 | tf_op jit(solution)/shard_map/ppermute | solution.py:757
  322.4 6.2 %collective-permute-start.42 = (f32[8,2304]{1,0:T(8,128)S(1)}, f32[8,2304]{1,0:T(8,128)S(1)}, u32[]{:S(2)}, u32[]{:S(2)}) collective-permute-start(f32[8,2304]{1,0:T(8,128)S(1)} %add.117), channel_id=1, source_target_pairs={{0,4},{1,5},{2,6},{3,7},{4,0},{5,1},{6,2},{7,3},{8,12},{9,13},{10,... | collective-permute-start | bytes 221192 | tf_op jit(solution)/shard_map/ppermute | solution.py:757
  328.2 27.5 %collective-permute-start.48 = (bf16[512,1024]{1,0:T(8,128)(2,1)}, bf16[512,1024]{1,0:T(8,128)(2,1)S(1)}, u32[]{:S(2)}, u32[]{:S(2)}) collective-permute-start(bf16[512,1024]{1,0:T(8,128)(2,1)} %late0_away.1), channel_id=1, source_target_pairs={{0,2},{1,3},{2,0},{3,1},{4,6},{5,7},{6,4},{7,5},{8,10},{9,11},{10,... | collective-permute-start | bytes 3145736 | tf_op jit(solution)/shard_map/ppermute | solution.py:757
  328.6 13.8 %collective-permute-start.43 = (f32[8,2304]{1,0:T(8,128)S(1)}, f32[8,2304]{1,0:T(8,128)S(1)}, u32[]{:S(2)}, u32[]{:S(2)}) collective-permute-start(f32[8,2304]{1,0:T(8,128)S(1)} %add.118), channel_id=1, source_target_pairs={{0,1},{1,0},{2,3},{3,2},{4,5},{5,4},{6,7},{7,6},{8,9},{9,8},{10,11... | collective-permute-start | bytes 221192 | tf_op jit(solution)/shard_map/ppermute | solution.py:757
  342.4 5.1 %collective-permute-start.44 = (f32[8,2304]{1,0:T(8,128)S(1)}, f32[8,2304]{1,0:T(8,128)S(1)}, u32[]{:S(2)}, u32[]{:S(2)}) collective-permute-start(f32[8,2304]{1,0:T(8,128)S(1)} %add.119), channel_id=1, source_target_pairs={{0,8},{1,9},{2,10},{3,11},{4,12},{5,13},{6,14},{7,15},{8,0},{9,1},... | collective-permute-start | bytes 221192 | tf_op jit(solution)/shard_map/ppermute | solution.py:757
  347.5 8.1 %collective-permute-start.45 = (f32[8,2304]{1,0:T(8,128)S(1)}, f32[8,2304]{1,0:T(8,128)S(1)}, u32[]{:S(2)}, u32[]{:S(2)}) collective-permute-start(f32[8,2304]{1,0:T(8,128)S(1)} %add.120), channel_id=1, source_target_pairs={{0,16},{1,17},{2,18},{3,19},{4,20},{5,21},{6,22},{7,23},{8,24},{9,... | collective-permute-start | bytes 221192 | tf_op jit(solution)/shard_map/ppermute | solution.py:757
  357.5 18.4 %collective-permute-start.49 = (bf16[2,2,2,32,1024]{4,3,1,0,2:T(8,128)(2,1)S(1)}, bf16[2,2,2,32,1024]{4,3,1,0,2:T(8,128)(2,1)S(1)}, u32[]{:S(2)}, u32[]{:S(2)}) collective-permute-start(bf16[2,2,2,32,1024]{4,3,1,0,2:T(8,128)(2,1)S(1)} %bitcast.89), channel_id=1, source_target_pairs={{0,4},{1,5},{2,6},{3,7},{4,0},{5,1},{6,2},{7,3},{8,12},{9,13},{10,... | collective-permute-start | bytes 1572872 | tf_op jit(solution)/shard_map/ppermute | solution.py:757
  359.3 49.9 %collective-permute-start.54 = (bf16[2,2,2,32,1408]{4,3,1,0,2:T(8,128)(2,1)S(1)}, bf16[2,2,2,32,1408]{4,3,1,0,2:T(8,128)(2,1)S(1)}, u32[]{:S(2)}, u32[]{:S(2)}) collective-permute-start(bf16[2,2,2,32,1408]{4,3,1,0,2:T(8,128)(2,1)S(1)} %bitcast.88), channel_id=1, source_target_pairs={{0,1},{1,0},{2,3},{3,2},{4,5},{5,4},{6,7},{7,6},{8,9},{9,8},{10,11... | collective-permute-start | bytes 2162696 | tf_op jit(solution)/shard_map/ppermute | solution.py:757
  376.1 39.1 %collective-permute-start.50 = (bf16[2,2,32,1024]{3,2,1,0:T(8,128)(2,1)S(1)}, bf16[2,2,32,1024]{3,2,1,0:T(8,128)(2,1)S(1)}, u32[]{:S(2)}, u32[]{:S(2)}) collective-permute-start(bf16[2,2,32,1024]{3,2,1,0:T(8,128)(2,1)S(1)} %dynamic-slice_bitcast_fusion.1), channel_id=1, source_target_pairs={{0,1},{1,0},{2,3},{3,2},{4,5},{5,4},{6,7},{7,6},{8,9},{9,8},{10,11... | collective-permute-start | bytes 786440 | tf_op jit(solution)/shard_map/ppermute | solution.py:757
  409.5 10.3 %collective-permute-start.55 = (bf16[2,2,32,1408]{3,2,1,0:T(8,128)(2,1)S(1)}, bf16[2,2,32,1408]{3,2,1,0:T(8,128)(2,1)S(1)}, u32[]{:S(2)}, u32[]{:S(2)}) collective-permute-start(bf16[2,2,32,1408]{3,2,1,0:T(8,128)(2,1)S(1)} %dynamic-slice_bitcast_fusion), channel_id=1, source_target_pairs={{0,4},{1,5},{2,6},{3,7},{4,0},{5,1},{6,2},{7,3},{8,12},{9,13},{10,... | collective-permute-start | bytes 1081352 | tf_op jit(solution)/shard_map/ppermute | solution.py:757
  415.3 11.8 %collective-permute-start.51 = (bf16[2,32,1024]{2,1,0:T(8,128)(2,1)S(1)}, bf16[2,32,1024]{2,1,0:T(8,128)(2,1)S(1)}, u32[]{:S(2)}, u32[]{:S(2)}) collective-permute-start(bf16[2,32,1024]{2,1,0:T(8,128)(2,1)S(1)} %dynamic-slice_bitcast_fusion.3), channel_id=1, source_target_pairs={{0,16},{1,17},{2,18},{3,19},{4,20},{5,21},{6,22},{7,23},{8,24},{9,... | collective-permute-start | bytes 393224 | tf_op jit(solution)/shard_map/ppermute | solution.py:757
  419.9 11.0 %collective-permute-start.56 = (bf16[2,32,1408]{2,1,0:T(8,128)(2,1)S(1)}, bf16[2,32,1408]{2,1,0:T(8,128)(2,1)S(1)}, u32[]{:S(2)}, u32[]{:S(2)}) collective-permute-start(bf16[2,32,1408]{2,1,0:T(8,128)(2,1)S(1)} %dynamic-slice_bitcast_fusion.2), channel_id=1, source_target_pairs={{0,16},{1,17},{2,18},{3,19},{4,20},{5,21},{6,22},{7,23},{8,24},{9,... | collective-permute-start | bytes 540680 | tf_op jit(solution)/shard_map/ppermute | solution.py:757
  427.1 5.1 %collective-permute-start.52 = (bf16[32,1024]{1,0:T(8,128)(2,1)S(1)}, bf16[32,1024]{1,0:T(8,128)(2,1)S(1)}, u32[]{:S(2)}, u32[]{:S(2)}) collective-permute-start(bf16[32,1024]{1,0:T(8,128)(2,1)S(1)} %dynamic-slice_bitcast_fusion.5), channel_id=1, source_target_pairs={{0,8},{1,9},{2,10},{3,11},{4,12},{5,13},{6,14},{7,15},{8,0},{9,1},... | collective-permute-start | bytes 196616 | tf_op jit(solution)/shard_map/ppermute | solution.py:757
  431.0 4.6 %collective-permute-start.57 = (bf16[32,1408]{1,0:T(8,128)(2,1)S(1)}, bf16[32,1408]{1,0:T(8,128)(2,1)S(1)}, u32[]{:S(2)}, u32[]{:S(2)}) collective-permute-start(bf16[32,1408]{1,0:T(8,128)(2,1)S(1)} %dynamic-slice_bitcast_fusion.4), channel_id=1, source_target_pairs={{0,8},{1,9},{2,10},{3,11},{4,12},{5,13},{6,14},{7,15},{8,0},{9,1},... | collective-permute-start | bytes 270344 | tf_op jit(solution)/shard_map/ppermute | solution.py:757
  (36 other events, 998.0 us)
Sparse Core Ops, SparseCore 0:
  10.9 85.4 all-gather.1
  296.4 114.8 reduce-scatter.1
